TPU v7x, 128 devices: a whole 4x4x4 slice. The times are simulated.
128 devices in a mesh: up: 8 (over x_lo, y), dn: 16 (over x_hi, z, core).
Axes of the slice: x: 4 (x_hi: 2, x_lo: 2; x = x_hi * 2 + x_lo), y: 4, z: 4, core: 2. Of those that a mesh axis runs over, the one named last changes fastest.
Arguments:
- coefficients: float32 [16384, 8192], P('up', 'dn'), may hold values from -6 to 6
- hopping_up: float32 [8, 128, 128], replicated, may hold values from -0.375 to 0.375
- partner_bits_up: int32 [7], replicated, may hold values from 0 to 6, each once
- block_signs_up: int32 [7, 128], replicated, may hold values from -2 to 2
- hopping_down: float32 [7, 128, 128], replicated, may hold values from -0.375 to 0.375
- partner_bits_down: int32 [6], replicated, may hold values from 0 to 5, each once
- block_signs_down: int32 [6, 64], replicated, may hold values from -2 to 2
- occupied_up: int32 [14, 16384], P(None, 'up'), may hold values 0 or 1
- occupied_down: int32 [14, 8192], P(None, 'dn'), may hold values 0 or 1
- site_energy: float32 [14], replicated, may hold values from 0.1 to 0.5
- repulsion: float32 [14], replicated, may hold values from 0.25 to 1
- energy_shift: float32 [], replicated, may hold values from -3 to -1
Outputs:
- residual: float32 [16384, 8192], P('up', 'dn')
- updated: float32 [16384, 8192], P('up', 'dn')
Inputs may be any that keep to these rules, and one draw needn't show every extreme that they name: `partner_bits_up`: each bit number of an up block appears exactly once. `partner_bits_down`: each bit number of a down block appears exactly once.
All inputs are finite; a program needn't handle non-finite values. No bound on the sum of `occupied_up` or of `occupied_down` on one device may be relied on, other than what follows from the above.
Results may differ from a plain program's by a relative error of at most 0.0001.
Values sent between devices are 32-bit elements; how exact they have to be, the bound alone decides.
No kernel may reach another device: no remote copies, remote signals or barrier semaphores. Data moves between devices by JAX's collectives and lax.ppermute only.
A program may use at most 192 MiB of HBM per device.

v0:
```python
import functools

import jax
import jax.numpy as jnp
from jax import lax
from jax.experimental import pallas as pl
from jax.experimental.pallas import tpu as pltpu
from jax.sharding import PartitionSpec as P

BLK = 128
CHUNKS = 4
WINDOW = 4
STEP = 256
MASKS = {
    "A": {"x": (4, 0), "y": (1, 0), "z": (0, 2)},
    "B": {"x": (4, 8), "y": (3, 0), "z": (0, 6)},
}
TURN = ("xyz", "yzx")
SMEM = pl.BlockSpec(memory_space=pltpu.SMEM)
F32 = jnp.float32
B16 = jnp.bfloat16


def whole(shape):
    return pl.BlockSpec(shape, lambda *_: (0,) * len(shape))


def params(mib):
    return pltpu.CompilerParams(vmem_limit_bytes=mib << 20)


def exchange(x, mask0, mask1):
    ups, dns = lax.axis_size("up"), lax.axis_size("dn")
    pairs = []
    for u in range(ups):
        for d in range(dns):
            mu, md = (mask0, mask1)[d % 2]
            pairs.append((u * dns + d, (u ^ mu) * dns + (d ^ md)))
    return lax.ppermute(x, ("up", "dn"), pairs)


def after(x, *others):
    return lax.optimization_barrier((x,) + others)[0]


def halves(x):
    hi = x.astype(B16)
    return hi, (x - hi.astype(F32)).astype(B16)


def thirds(x):
    hi = x.astype(B16).astype(F32)
    mid = (x - hi).astype(B16).astype(F32)
    return hi, mid, (x - hi - mid).astype(B16).astype(F32)


def dot(a, b):
    return jnp.dot(a, b, preferred_element_type=F32)


def prepare(inv_up, inv_dn, sign_dn, dn_order, hop_up, hop_dn, occ_up, occ_dn, site, rep,
            up_w, loc_w, rem_w, left, right):
    for slot in range(8):
        h = hop_up[0] if slot == 0 else hop_up[1 + inv_up[slot - 1]]
        hi, lo = halves(h)
        up_w[slot, :BLK, :] = hi
        up_w[slot, BLK:, :] = lo
    loc_w[...] = jnp.zeros_like(loc_w)
    hi, lo = halves(hop_dn[0].T)
    for q in range(4):
        loc_w[q * BLK:(q + 1) * BLK, q * BLK:(q + 1) * BLK] = hi
        loc_w[q * BLK:(q + 1) * BLK, 512 + q * BLK:512 + (q + 1) * BLK] = lo
    for bit in range(2):
        h = hop_dn[1 + inv_dn[bit]].T
        for q in range(4):
            hi, lo = halves(h)
            s = sign_dn[bit, q]
            k = q ^ (1 << bit)
            hi = (hi.astype(F32) * s).astype(B16)
            lo = (lo.astype(F32) * s).astype(B16)
            loc_w[k * BLK:(k + 1) * BLK, q * BLK:(q + 1) * BLK] = hi
            loc_w[k * BLK:(k + 1) * BLK, 512 + q * BLK:512 + (q + 1) * BLK] = lo
    for t in range(4):
        bit = dn_order[t]
        h = hop_dn[1 + inv_dn[bit]].T
        for q in range(4):
            hi, lo = halves(h)
            s = sign_dn[bit, q]
            rem_w[q, t * BLK:(t + 1) * BLK, :BLK] = (hi.astype(F32) * s).astype(B16)
            rem_w[q, t * BLK:(t + 1) * BLK, BLK:] = (lo.astype(F32) * s).astype(B16)
    ou, od = occ_up[...], occ_dn[...]
    sites = thirds(site[...])
    reps = thirds(rep[...])
    for n in range(3):
        left[16 * n:16 * n + 16, :] = (reps[n] * ou).astype(B16)
        right[16 * n:16 * n + 16, :] = od.astype(B16)
        left[48 + 16 * n:64 + 16 * n, :] = (sites[n] * ou).astype(B16)
        right[48 + 16 * n:64 + 16 * n, :] = jnp.ones_like(od).astype(B16)
        left[96 + 16 * n:112 + 16 * n, :] = jnp.ones_like(ou).astype(B16)
        right[96 + 16 * n:112 + 16 * n, :] = (sites[n] * od).astype(B16)


def signed(up_w, slot, s):
    return (up_w[slot].astype(F32) * s).astype(B16)


def local_body(sign_up, own, near, far, up_w, loc_w, out):
    i = pl.program_id(0)
    own_hi, own_lo = halves(own[...])
    near_hi, near_lo = halves(near[...])
    far_hi, far_lo = halves(far[...])
    width = loc_w.shape[0]

    def rows(x, p):
        return x[p * BLK:(p + 1) * BLK]

    across = dot(own_hi, loc_w[...])
    across = across[:, :width] + across[:, width:] + dot(own_lo, loc_w[:, :width])
    for p in range(4):
        w = [up_w[0]] + [signed(up_w, 1 + b, sign_up[b, 4 * i + p]) for b in range(4)]
        w = jnp.concatenate(w, axis=1)

        def stack(o, n, f):
            return jnp.concatenate(
                [rows(o, p), rows(o, p ^ 1), rows(o, p ^ 2), rows(n, p), rows(f, p)], axis=0
            )

        r = dot(w, stack(own_hi, near_hi, far_hi))
        r = r[:BLK] + r[BLK:] + dot(w[:BLK], stack(own_lo, near_lo, far_lo))
        out[p * BLK:(p + 1) * BLK, :] = r + rows(across, p)


def final_body(first, which, sign_up, slots, shift, a0, a1, a2, b0, b1, b2, mate, acc, own, up_w, rem_w,
               left, right, *rest):
    residual, updated = rest[-2:]
    zero = which[0] == 0
    step = pl.program_id(0)
    ups = [a0[...], jnp.where(zero, a1[...], a2[...]), jnp.where(zero, b1[...], b0[...])]
    dns = [jnp.where(zero, a2[...], a1[...]), jnp.where(zero, b0[...], b1[...]), b2[...], mate[...]]
    total = acc[...]
    up_parts = [halves(x) for x in ups]
    dn_parts = [halves(x) for x in dns]
    columns = []
    for q in range(4):
        cut = slice(q * BLK, (q + 1) * BLK)
        hi = jnp.concatenate([x[0][:, cut] for x in dn_parts], axis=1)
        lo = jnp.concatenate([x[1][:, cut] for x in dn_parts], axis=1)
        r = dot(hi, rem_w[q])
        columns.append(r[:, :BLK] + r[:, BLK:] + dot(lo, rem_w[q, :, :BLK]))
    total = total + jnp.concatenate(columns, axis=1)
    blocks = []
    for p in range(STEP // BLK):
        cut = slice(p * BLK, (p + 1) * BLK)
        block = first + step * (STEP // BLK) + p
        w = jnp.concatenate(
            [signed(up_w, slots[t], sign_up[slots[t] - 1, block]) for t in range(3)], axis=1
        )
        r = dot(w, jnp.concatenate([x[0][cut] for x in up_parts], axis=0))
        blocks.append(
            r[:BLK] + r[BLK:] + dot(w[:BLK], jnp.concatenate([x[1][cut] for x in up_parts], axis=0))
        )
    total = total + jnp.concatenate(blocks, axis=0)
    gap = lax.dot_general(left[...], right[...], (((0,), (0,)), ((), ())),
                          preferred_element_type=F32) - shift[0]
    c = own[...]
    res = total + gap * c
    residual[...] = res
    updated[...] = c - res / gap


def shards(
    coefficients,
    hopping_up,
    partner_bits_up,
    block_signs_up,
    hopping_down,
    partner_bits_down,
    block_signs_down,
    occupied_up,
    occupied_down,
    site_energy,
    repulsion,
    energy_shift,
):
    rows, width = coefficients.shape
    size = rows // CHUNKS
    up_local, dn_local = rows // BLK, width // BLK
    core = lax.axis_index("dn") % 2

    def by_bit(bits, signs, first, count):
        number = bits.shape[0]
        chosen = bits[None, :] == jnp.arange(number)[:, None]
        place = jnp.sum(jnp.where(chosen, jnp.arange(number)[None, :], 0), axis=1).astype(jnp.int32)
        part = lax.dynamic_slice_in_dim(signs, first, count, axis=1)
        return place, jnp.sum(jnp.where(chosen[:, :, None], part[None], 0), axis=1).astype(F32)

    inv_up, sign_up = by_bit(partner_bits_up, block_signs_up, lax.axis_index("up") * up_local, up_local)
    inv_dn, sign_dn = by_bit(partner_bits_down, block_signs_down, lax.axis_index("dn") * dn_local, dn_local)
    slots = jnp.where(core == 0, jnp.array([7, 5, 6], jnp.int32), jnp.array([5, 7, 6], jnp.int32))
    dn_order = jnp.where(core == 0, jnp.array([3, 5, 4, 2], jnp.int32), jnp.array([3, 4, 5, 2], jnp.int32))
    which = core.astype(jnp.int32).reshape(1)

    mate = exchange(coefficients, (0, 1), (0, 1))
    order = [("A", j, 0) for j in range(3)]
    for i in range(CHUNKS):
        for j in range(3):
            order.append(("B", j, i))
            if i + 1 < CHUNKS:
                order.append(("A", j, i + 1))
    got, done = {}, []
    for n, (kind, j, i) in enumerate(order):
        if kind == "A":
            source = coefficients if n < WINDOW else after(coefficients, done[n - WINDOW])
            source = lax.slice_in_dim(source, i * size, (i + 1) * size)
        else:
            source = got["A", j, i]
            if n >= WINDOW:
                source = after(source, done[n - WINDOW])
        got[kind, j, i] = exchange(source, MASKS[kind][TURN[0][j]], MASKS[kind][TURN[1][j]])
        done.append(got[kind, j, i])

    pad = ((0, 2), (0, 0))
    up_w, loc_w, rem_w, left, right = pl.pallas_call(
        prepare,
        out_shape=[
            jax.ShapeDtypeStruct((8, 2 * BLK, BLK), B16),
            jax.ShapeDtypeStruct((width, 2 * width), B16),
            jax.ShapeDtypeStruct((4, 4 * BLK, 2 * BLK), B16),
            jax.ShapeDtypeStruct((144, rows), B16),
            jax.ShapeDtypeStruct((144, width), B16),
        ],
        in_specs=[SMEM] * 4 + [pl.BlockSpec(memory_space=pltpu.VMEM)] * 6,
        compiler_params=params(24),
        cost_estimate=pl.CostEstimate(flops=0, bytes_accessed=8 << 20, transcendentals=0),
        name="prepare",
    )(
        inv_up, inv_dn, sign_dn, dn_order, hopping_up, hopping_down,
        jnp.pad(occupied_up.astype(F32), pad), jnp.pad(occupied_down.astype(F32), pad),
        jnp.pad(site_energy[:, None], pad), jnp.pad(repulsion[:, None], pad),
    )

    block = (size, width)
    acc = pl.pallas_call(
        local_body,
        grid=(CHUNKS,),
        out_shape=jax.ShapeDtypeStruct((rows, width), F32),
        in_specs=[
            SMEM,
            pl.BlockSpec(block, lambda i: (i, 0)),
            pl.BlockSpec(block, lambda i: (i ^ 1, 0)),
            pl.BlockSpec(block, lambda i: (i ^ 2, 0)),
            whole(up_w.shape),
            whole(loc_w.shape),
        ],
        out_specs=pl.BlockSpec(block, lambda i: (i, 0)),
        compiler_params=params(36),
        cost_estimate=pl.CostEstimate(flops=12 << 30, bytes_accessed=24 << 20, transcendentals=0),
        name="local",
    )(sign_up, coefficients, coefficients, coefficients, up_w, loc_w)

    outs = None
    tile = (STEP, width)
    steps = size // STEP
    for i in range(CHUNKS):
        base = i * steps
        here = pl.BlockSpec(tile, lambda s: (s, 0))
        there = pl.BlockSpec(tile, lambda s, base=base: (base + s, 0))
        arrived = [got[k, j, i] for k in "AB" for j in range(3)]
        extra = [] if outs is None else list(outs)
        operands = [which, sign_up, slots, energy_shift.reshape(1), *arrived, mate, acc, coefficients,
                    up_w, rem_w, left, right]
        outs = pl.pallas_call(
            functools.partial(final_body, i * (size // BLK)),
            grid=(steps,),
            out_shape=[jax.ShapeDtypeStruct((rows, width), F32)] * 2,
            in_specs=[SMEM] * 4 + [here] * 6 + [there] * 3 + [
                whole(up_w.shape),
                whole(rem_w.shape),
                pl.BlockSpec((144, STEP), lambda s, base=base: (0, base + s)),
                whole(right.shape),
            ] + [pl.BlockSpec(memory_space=pl.ANY)] * len(extra),
            out_specs=[there, there],
            input_output_aliases={len(operands): 0, len(operands) + 1: 1} if extra else {},
            compiler_params=params(36),
            cost_estimate=pl.CostEstimate(flops=3 << 30, bytes_accessed=12 << 20, transcendentals=0),
            name="finish",
        )(*operands, *extra)
    return tuple(outs)


def solution(mesh):
    placed = (
        P("up", "dn"),
        P(),
        P(),
        P(),
        P(),
        P(),
        P(),
        P(None, "up"),
        P(None, "dn"),
        P(),
        P(),
        P(),
    )
    return jax.shard_map(
        shards,
        mesh=mesh,
        in_specs=placed,
        out_specs=(P("up", "dn"), P("up", "dn")),
        check_vma=False,
    )
```

profile of v0, /device:TPU:16, one launch (start us, length us, event | category | flops | bytes accessed | tf_op | source)
XLA Modules:
  0.0 156.5 jit_solution(2966537529623550759)
XLA Ops:
  0.6 1.3 slice.32
  1.9 1.6 %collective-permute-start = (f32[512,512]{1,0:T(8,128)S(1)}, f32[512,512]{1,0:T(8,128)S(1)}, u32[]{:S(2)}, u32[]{:S(2)}) collective-permute-start(f32[512,512]{1,0:T(8,128)S(1)} %slice.32), channel_id=1, source_target_pairs={{0,64},{1,17},{2,66},{3,19},{4,68},{5,21},{6,70},{7,23},{8,72},{9,... | collective-permute-start | bytes 3145736 | tf_op jit(solution)/shard_map/ppermute | solution.py:39
  3.5 1.3 collective-permute-start.11
  4.8 1.9 %collective-permute-start.5 = (f32[512,512]{1,0:T(8,128)S(1)}, f32[512,512]{1,0:T(8,128)S(1)}, u32[]{:S(2)}, u32[]{:S(2)}) collective-permute-start(f32[512,512]{1,0:T(8,128)S(1)} %slice.32), channel_id=1, source_target_pairs={{0,2},{1,65},{2,0},{3,67},{4,6},{5,69},{6,4},{7,71},{8,10},{9,73},... | collective-permute-start | bytes 3145736 | tf_op jit(solution)/shard_map/ppermute | solution.py:39
  6.7 19.8 %collective-permute-done.a0 = f32[512,512]{1,0:T(8,128)S(1)} collective-permute-done((f32[512,512]{1,0:T(8,128)S(1)}, f32[512,512]{1,0:T(8,128)S(1)}, u32[]{:S(2)}, u32[]{:S(2)}) %collective-permute-start) | collective-permute-done | bytes 1048608 | tf_op jit(solution)/shard_map/ppermute | solution.py:39
  26.5 2.8 %collective-permute-start.18 = (f32[512,512]{1,0:T(8,128)S(1)}, f32[512,512]{1,0:T(8,128)S(1)}, u32[]{:S(2)}, u32[]{:S(2)}) collective-permute-start(f32[512,512]{1,0:T(8,128)S(1)} %collective-permute-done.a0), channel_id=1, source_target_pairs={{0,72},{1,49},{2,74},{3,51},{4,76},{5,53},{6,78},{7,55},{8,64},{9,... | collective-permute-start | bytes 3145736 | tf_op jit(solution)/shard_map/ppermute | solution.py:39
  29.2 1.3 slice.33
  30.9 1.4 collective-permute-start.12
  32.3 1.3 slice.37
  34.1 8.4 %collective-permute-done.18.b0 = f32[512,512]{1,0:T(8,128)S(1)} collective-permute-done((f32[512,512]{1,0:T(8,128)S(1)}, f32[512,512]{1,0:T(8,128)S(1)}, u32[]{:S(2)}, u32[]{:S(2)}) %collective-permute-start.18) | collective-permute-done | bytes 1048608 | tf_op jit(solution)/shard_map/ppermute | solution.py:39
  42.5 5.6 %collective-permute-start.19 = (f32[512,512]{1,0:T(8,128)S(1)}, f32[512,512]{1,0:T(8,128)S(1)}, u32[]{:S(2)}, u32[]{:S(2)}) collective-permute-start(f32[512,512]{1,0:T(8,128)S(1)} %collective-permute-done.5.a2), channel_id=1, source_target_pairs={{0,6},{1,73},{2,4},{3,75},{4,2},{5,77},{6,0},{7,79},{8,14},{9,65},... | collective-permute-start | bytes 3145736 | tf_op jit(solution)/shard_map/ppermute | solution.py:39
  48.1 1.3 slice.34
  49.5 0.9 collective-permute-start.2
  50.4 2.4 %collective-permute-start.13 = (f32[512,512]{1,0:T(8,128)}, f32[512,512]{1,0:T(8,128)}, u32[]{:S(2)}, u32[]{:S(2)}) collective-permute-start(f32[512,512]{1,0:T(8,128)} %collective-permute-done.1.a0), channel_id=1, source_target_pairs={{0,72},{1,49},{2,74},{3,51},{4,76},{5,53},{6,78},{7,55},{8,64},{9,... | collective-permute-start | bytes 3145736 | tf_op jit(solution)/shard_map/ppermute | solution.py:39
  52.8 2.3 %slice.38 = f32[512,512]{1,0:T(8,128)} slice(f32[2048,512]{1,0:T(8,128)} %own.9), slice={[1024:1536], [0:512]} | slice | bytes 2097152 | tf_op jit(solution)/shard_map/slice | solution.py:214
  55.1 0.7 collective-permute-start.7
  55.8 5.1 %collective-permute-done.19.b2 = f32[512,512]{1,0:T(8,128)S(1)} collective-permute-done((f32[512,512]{1,0:T(8,128)S(1)}, f32[512,512]{1,0:T(8,128)S(1)}, u32[]{:S(2)}, u32[]{:S(2)}) %collective-permute-start.19) | collective-permute-done | bytes 1048608 | tf_op jit(solution)/shard_map/ppermute | solution.py:39
  60.9 1.0 copy-done.5
  61.9 2.5 %collective-permute-done.2.a2 = f32[512,512]{1,0:T(8,128)S(1)} collective-permute-done((f32[512,512]{1,0:T(8,128)S(1)}, f32[512,512]{1,0:T(8,128)S(1)}, u32[]{:S(2)}, u32[]{:S(2)}) %collective-permute-start.2) | collective-permute-done | bytes 1048608 | tf_op jit(solution)/shard_map/ppermute | solution.py:39
  64.4 1.0 copy-done.7
  65.4 2.3 %slice.35 = f32[512,512]{1,0:T(8,128)} slice(f32[2048,512]{1,0:T(8,128)} %own.9), slice={[1024:1536], [0:512]} | slice | bytes 2097152 | tf_op jit(solution)/shard_map/slice | solution.py:214
  67.6 0.8 collective-permute-start.3
  68.4 2.8 %collective-permute-done.13.b0 = f32[512,512]{1,0:T(8,128)} collective-permute-done((f32[512,512]{1,0:T(8,128)}, f32[512,512]{1,0:T(8,128)}, u32[]{:S(2)}, u32[]{:S(2)}) %collective-permute-start.13) | collective-permute-done | bytes 1048608 | tf_op jit(solution)/shard_map/ppermute | solution.py:39
  71.2 2.5 %collective-permute-start.14 = (f32[512,512]{1,0:T(8,128)}, f32[512,512]{1,0:T(8,128)}, u32[]{:S(2)}, u32[]{:S(2)}) collective-permute-start(f32[512,512]{1,0:T(8,128)} %copy-done.7), channel_id=1, source_target_pairs={{0,6},{1,73},{2,4},{3,75},{4,2},{5,77},{6,0},{7,79},{8,14},{9,65},... | collective-permute-start | bytes 3145736 | tf_op jit(solution)/shard_map/ppermute | solution.py:39
  74.1 2.3 %slice.39 = f32[512,512]{1,0:T(8,128)} slice(f32[2048,512]{1,0:T(8,128)} %own.9), slice={[1024:1536], [0:512]} | slice | bytes 2097152 | tf_op jit(solution)/shard_map/slice | solution.py:214
  77.0 3.0 %collective-permute-start.21 = (f32[512,512]{1,0:T(8,128)}, f32[512,512]{1,0:T(8,128)}, u32[]{:S(2)}, u32[]{:S(2)}) collective-permute-start(f32[512,512]{1,0:T(8,128)} %collective-permute-done.7.a0), channel_id=1, source_target_pairs={{0,72},{1,49},{2,74},{3,51},{4,76},{5,53},{6,78},{7,55},{8,64},{9,... | collective-permute-start | bytes 3145736 | tf_op jit(solution)/shard_map/ppermute | solution.py:39
  79.9 2.8 %collective-permute-done.3.a1 = f32[512,512]{1,0:T(8,128)} collective-permute-done((f32[512,512]{1,0:T(8,128)}, f32[512,512]{1,0:T(8,128)}, u32[]{:S(2)}, u32[]{:S(2)}) %collective-permute-start.3) | collective-permute-done | bytes 1048608 | tf_op jit(solution)/shard_map/ppermute | solution.py:39
  82.7 2.3 %slice.36 = f32[512,512]{1,0:T(8,128)} slice(f32[2048,512]{1,0:T(8,128)} %own.9), slice={[1536:2048], [0:512]} | slice | bytes 2097152 | tf_op jit(solution)/shard_map/slice | solution.py:214
  87.1 1.0 copy-done.9
  88.1 1.0 copy-done.10
  89.1 1.1 prepare.1
  90.2 1.8 %collective-permute-done.14.b2 = f32[512,512]{1,0:T(8,128)} collective-permute-done((f32[512,512]{1,0:T(8,128)}, f32[512,512]{1,0:T(8,128)}, u32[]{:S(2)}, u32[]{:S(2)}) %collective-permute-start.14) | collective-permute-done | bytes 1048608 | tf_op jit(solution)/shard_map/ppermute | solution.py:39
  92.2 3.3 %collective-permute-done.8.a2 = f32[512,512]{1,0:T(8,128)} collective-permute-done((f32[512,512]{1,0:T(8,128)}, f32[512,512]{1,0:T(8,128)}, u32[]{:S(2)}, u32[]{:S(2)}) %collective-permute-start.8) | collective-permute-done | bytes 1048608 | tf_op jit(solution)/shard_map/ppermute | solution.py:39
  95.5 1.3 slice.40
  96.8 3.4 %collective-permute-start.9 = (f32[512,512]{1,0:T(8,128)S(1)}, f32[512,512]{1,0:T(8,128)S(1)}, u32[]{:S(2)}, u32[]{:S(2)}) collective-permute-start(f32[512,512]{1,0:T(8,128)S(1)} %slice.40), channel_id=1, source_target_pairs={{0,16},{1,3},{2,18},{3,1},{4,20},{5,7},{6,22},{7,5},{8,24},{9,11},... | collective-permute-start | bytes 3145736 | tf_op jit(solution)/shard_map/ppermute | solution.py:39
  100.2 0.9 collective-permute-start.22
  101.1 1.2 collective-permute-done.4.a0
  102.3 1.3 slice.41
  104.0 11.2 %local.1.acc = f32[2048,512]{1,0:T(8,128)S(1)} custom-call(f32[7,16]{1,0:T(8,128)S(1)} %convert_element_type.19.sign_up, f32[2048,512]{1,0:T(8,128)} %own.9, f32[2048,512]{1,0:T(8,128)} %own.9, f32[2048,512]{1,0:T(8,128)} %own.9, bf16[8,256,128]{2,1,0:T(8,128)(2,1)S(1)} %get-tuple-element.53.up_w, bf16[512,1024]{1,0:T(8,128)(2,1)S(1)} %get-tuple-element.54.loc_w), custom_call_target="tpu_custom_call" | custom-call | flops 12884901888 | bytes 25165824 | tf_op jit(solution)/shard_map/local/pallas_call | solution.py:243
  115.2 0.7 collective-permute-start.16
  115.9 2.4 %collective-permute-done.9.a1 = f32[512,512]{1,0:T(8,128)S(1)} collective-permute-done((f32[512,512]{1,0:T(8,128)S(1)}, f32[512,512]{1,0:T(8,128)S(1)}, u32[]{:S(2)}, u32[]{:S(2)}) %collective-permute-start.9) | collective-permute-done | bytes 1048608 | tf_op jit(solution)/shard_map/ppermute | solution.py:39
  118.3 7.7 %collective-permute-done.22.b2 = f32[512,512]{1,0:T(8,128)S(1)} collective-permute-done((f32[512,512]{1,0:T(8,128)}, f32[512,512]{1,0:T(8,128)S(1)}, u32[]{:S(2)}, u32[]{:S(2)}) %collective-permute-start.22) | collective-permute-done | bytes 1048608 | tf_op jit(solution)/shard_map/ppermute | solution.py:39
  126.0 2.9 %collective-permute-start.23 = (f32[512,512]{1,0:T(8,128)S(1)}, f32[512,512]{1,0:T(8,128)S(1)}, u32[]{:S(2)}, u32[]{:S(2)}) collective-permute-start(f32[512,512]{1,0:T(8,128)S(1)} %collective-permute-done.10.a2), channel_id=1, source_target_pairs={{0,6},{1,73},{2,4},{3,75},{4,2},{5,77},{6,0},{7,79},{8,14},{9,65},... | collective-permute-start | bytes 3145736 | tf_op jit(solution)/shard_map/ppermute | solution.py:39
  129.0 5.1 %finish.4 = (f32[2048,512]{1,0:T(8,128)}, f32[2048,512]{1,0:T(8,128)}) custom-call(s32[1]{0:T(128)} %bitcast.which, f32[7,16]{1,0:T(8,128)S(1)} %convert_element_type.19.sign_up, s32[3]{0:T(128)S(1)} %broadcast_select_fusion.1.slots, f32[1]{0:T(128)} %bitcast.4.shift, f32[512,512]{1,0:T(8,128)S(1)} %collective-permute-done.a0, ...), custom_call_target="tpu_custom_call" | custom-call | flops 3221225472 | bytes 12582912 | tf_op jit(solution)/shard_map/finish/pallas_call | solution.py:272
  134.0 5.7 %finish.5 = (f32[2048,512]{1,0:T(8,128)}, f32[2048,512]{1,0:T(8,128)}) custom-call(s32[1]{0:T(128)} %bitcast.which, f32[7,16]{1,0:T(8,128)S(1)} %convert_element_type.19.sign_up, s32[3]{0:T(128)S(1)} %broadcast_select_fusion.1.slots, f32[1]{0:T(128)} %bitcast.5.shift, ...), custom_call_target="tpu_custom_call", output_to_operand_aliasing={{0}: (17, {}), {1}: (18, {})} | custom-call | flops 3221225472 | bytes 12582912 | tf_op jit(solution)/shard_map/finish/pallas_call | solution.py:272
  139.7 5.5 %finish.6 = (f32[2048,512]{1,0:T(8,128)}, f32[2048,512]{1,0:T(8,128)}) custom-call(s32[1]{0:T(128)} %bitcast.which, f32[7,16]{1,0:T(8,128)S(1)} %convert_element_type.19.sign_up, s32[3]{0:T(128)S(1)} %broadcast_select_fusion.1.slots, f32[1]{0:T(128)} %bitcast.6.shift, ...), custom_call_target="tpu_custom_call", output_to_operand_aliasing={{0}: (17, {}), {1}: (18, {})} | custom-call | flops 3221225472 | bytes 12582912 | tf_op jit(solution)/shard_map/finish/pallas_call | solution.py:272
  145.2 6.2 %collective-permute-done.23.b2 = f32[512,512]{1,0:T(8,128)S(1)} collective-permute-done((f32[512,512]{1,0:T(8,128)S(1)}, f32[512,512]{1,0:T(8,128)S(1)}, u32[]{:S(2)}, u32[]{:S(2)}) %collective-permute-start.23) | collective-permute-done | bytes 1048608 | tf_op jit(solution)/shard_map/ppermute | solution.py:39
  151.5 5.0 %finish.7 = (f32[2048,512]{1,0:T(8,128)}, f32[2048,512]{1,0:T(8,128)}) custom-call(s32[1]{0:T(128)} %bitcast.which, f32[7,16]{1,0:T(8,128)S(1)} %convert_element_type.19.sign_up, s32[3]{0:T(128)S(1)} %broadcast_select_fusion.1.slots, f32[1]{0:T(128)} %bitcast.7.shift, ...), custom_call_target="tpu_custom_call", output_to_operand_aliasing={{0}: (17, {}), {1}: (18, {})} | custom-call | flops 3221225472 | bytes 12582912 | tf_op jit(solution)/shard_map/finish/pallas_call | solution.py:272
  (83 shorter events, 3.9 us)
Async XLA Ops:
  0.6 85.3 %copy-start = (s32[7,128]{1,0:T(8,128)S(1)}, s32[7,128]{1,0:T(8,128)}, u32[]{:S(2)}) copy-start(s32[7,128]{1,0:T(8,128)} %param.19) | copy-start | bytes 10756
  1.9 24.5 %collective-permute-start = (f32[512,512]{1,0:T(8,128)S(1)}, f32[512,512]{1,0:T(8,128)S(1)}, u32[]{:S(2)}, u32[]{:S(2)}) collective-permute-start(f32[512,512]{1,0:T(8,128)S(1)} %slice.32), channel_id=1, source_target_pairs={{0,64},{1,17},{2,66},{3,19},{4,68},{5,21},{6,70},{7,23},{8,72},{9,... | collective-permute-start | bytes 3145736 | tf_op jit(solution)/shard_map/ppermute | solution.py:39
  3.5 27.3 %collective-permute-start.11 = (f32[512,512]{1,0:T(8,128)S(1)}, f32[512,512]{1,0:T(8,128)S(1)}, u32[]{:S(2)}, u32[]{:S(2)}) collective-permute-start(f32[512,512]{1,0:T(8,128)S(1)} %slice.32), channel_id=1, source_target_pairs={{0,16},{1,3},{2,18},{3,1},{4,20},{5,7},{6,22},{7,5},{8,24},{9,11},... | collective-permute-start | bytes 3145736 | tf_op jit(solution)/shard_map/ppermute | solution.py:39
  4.8 27.5 %collective-permute-start.5 = (f32[512,512]{1,0:T(8,128)S(1)}, f32[512,512]{1,0:T(8,128)S(1)}, u32[]{:S(2)}, u32[]{:S(2)}) collective-permute-start(f32[512,512]{1,0:T(8,128)S(1)} %slice.32), channel_id=1, source_target_pairs={{0,2},{1,65},{2,0},{3,67},{4,6},{5,69},{6,4},{7,71},{8,10},{9,73},... | collective-permute-start | bytes 3145736 | tf_op jit(solution)/shard_map/ppermute | solution.py:39
  26.5 16.0 %collective-permute-start.18 = (f32[512,512]{1,0:T(8,128)S(1)}, f32[512,512]{1,0:T(8,128)S(1)}, u32[]{:S(2)}, u32[]{:S(2)}) collective-permute-start(f32[512,512]{1,0:T(8,128)S(1)} %collective-permute-done.a0), channel_id=1, source_target_pairs={{0,72},{1,49},{2,74},{3,51},{4,76},{5,53},{6,78},{7,55},{8,64},{9,... | collective-permute-start | bytes 3145736 | tf_op jit(solution)/shard_map/ppermute | solution.py:39
  30.5 37.8 %copy-start.20 = (s32[6]{0:T(128)S(1)}, s32[6]{0:T(128)}, u32[]{:S(2)}) copy-start(s32[6]{0:T(128)} %param.21) | copy-start | bytes 76
  30.6 17.5 %collective-permute-start.1 = (f32[512,512]{1,0:T(8,128)S(1)}, f32[512,512]{1,0:T(8,128)}, u32[]{:S(2)}, u32[]{:S(2)}) collective-permute-start(f32[512,512]{1,0:T(8,128)S(1)} %slice.33), channel_id=1, source_target_pairs={{0,64},{1,17},{2,66},{3,19},{4,68},{5,21},{6,70},{7,23},{8,72},{9,... | collective-permute-start | bytes 3145736 | tf_op jit(solution)/shard_map/ppermute | solution.py:39
  30.9 19.5 %collective-permute-start.12 = (f32[512,512]{1,0:T(8,128)S(1)}, f32[512,512]{1,0:T(8,128)S(1)}, u32[]{:S(2)}, u32[]{:S(2)}) collective-permute-start(f32[512,512]{1,0:T(8,128)S(1)} %collective-permute-done.11.a1), channel_id=1, source_target_pairs={{0,48},{1,7},{2,50},{3,5},{4,52},{5,3},{6,54},{7,1},{8,56},{9,15},... | collective-permute-start | bytes 3145736 | tf_op jit(solution)/shard_map/ppermute | solution.py:39
  33.6 19.3 %collective-permute-start.6 = (f32[512,512]{1,0:T(8,128)S(1)}, f32[512,512]{1,0:T(8,128)}, u32[]{:S(2)}, u32[]{:S(2)}) collective-permute-start(f32[512,512]{1,0:T(8,128)S(1)} %slice.37), channel_id=1, source_target_pairs={{0,16},{1,3},{2,18},{3,1},{4,20},{5,7},{6,22},{7,5},{8,24},{9,11},... | collective-permute-start | bytes 3145736 | tf_op jit(solution)/shard_map/ppermute | solution.py:39
  42.5 18.4 %copy-start.1 = (f32[512,512]{1,0:T(8,128)}, f32[512,512]{1,0:T(8,128)S(1)}, u32[]{:S(2)}) copy-start(f32[512,512]{1,0:T(8,128)S(1)} %collective-permute-done.18.b0) | copy-start | bytes 3145732
  42.5 18.4 %collective-permute-start.19 = (f32[512,512]{1,0:T(8,128)S(1)}, f32[512,512]{1,0:T(8,128)S(1)}, u32[]{:S(2)}, u32[]{:S(2)}) collective-permute-start(f32[512,512]{1,0:T(8,128)S(1)} %collective-permute-done.5.a2), channel_id=1, source_target_pairs={{0,6},{1,73},{2,4},{3,75},{4,2},{5,77},{6,0},{7,79},{8,14},{9,65},... | collective-permute-start | bytes 3145736 | tf_op jit(solution)/shard_map/ppermute | solution.py:39
  49.4 35.9 %copy-start.13 = (s32[6,64]{1,0:T(8,128)S(1)}, s32[6,64]{1,0:T(8,128)}, u32[]{:S(2)}) copy-start(s32[6,64]{1,0:T(8,128)} %param.22) | copy-start | bytes 4612
  49.4 36.2 %copy-start.11 = (s32[14,2048]{1,0:T(8,128)S(1)}, s32[14,2048]{1,0:T(8,128)}, u32[]{:S(2)}) copy-start(s32[14,2048]{1,0:T(8,128)} %param.23) | copy-start | bytes 344068
  49.4 36.2 %copy-start.12 = (s32[14,512]{1,0:T(8,128)S(1)}, s32[14,512]{1,0:T(8,128)}, u32[]{:S(2)}) copy-start(s32[14,512]{1,0:T(8,128)} %param.24) | copy-start | bytes 86020
  49.4 36.3 %copy-start.14 = (f32[14]{0:T(128)S(1)}, f32[14]{0:T(128)}, u32[]{:S(2)}) copy-start(f32[14]{0:T(128)} %param.25) | copy-start | bytes 172
  49.5 36.4 %copy-start.15 = (f32[14]{0:T(128)S(1)}, f32[14]{0:T(128)}, u32[]{:S(2)}) copy-start(f32[14]{0:T(128)} %param.26) | copy-start | bytes 172
  49.5 36.6 %copy-start.21 = (s32[7]{0:T(128)S(1)}, s32[7]{0:T(128)}, u32[]{:S(2)}) copy-start(s32[7]{0:T(128)} %param.18) | copy-start | bytes 88
  49.5 37.6 %copy-start.18 = (s32[4]{0:T(128)S(1)}, s32[4]{0:T(128)}, u32[]{:S(2)}) copy-start(s32[4]{0:T(128)} %constant.43.clone) | copy-start | bytes 52
  49.5 37.5 %copy-start.19 = (s32[4]{0:T(128)S(1)}, s32[4]{0:T(128)}, u32[]{:S(2)}) copy-start(s32[4]{0:T(128)} %constant.44.clone) | copy-start | bytes 52
  49.5 14.9 %collective-permute-start.2 = (f32[512,512]{1,0:T(8,128)S(1)}, f32[512,512]{1,0:T(8,128)S(1)}, u32[]{:S(2)}, u32[]{:S(2)}) collective-permute-start(f32[512,512]{1,0:T(8,128)S(1)} %slice.34), channel_id=1, source_target_pairs={{0,2},{1,65},{2,0},{3,67},{4,6},{5,69},{6,4},{7,71},{8,10},{9,73},... | collective-permute-start | bytes 3145736 | tf_op jit(solution)/shard_map/ppermute | solution.py:39
  50.4 78.6 %collective-permute-start.24 = (f32[2048,512]{1,0:T(8,128)}, f32[2048,512]{1,0:T(8,128)}, u32[]{:S(2)}, u32[]{:S(2)}) collective-permute-start(f32[2048,512]{1,0:T(8,128)} %own.9), channel_id=1, source_target_pairs={{0,1},{1,0},{2,3},{3,2},{4,5},{5,4},{6,7},{7,6},{8,9},{9,8},{10,11... | collective-permute-start | bytes 12582920 | tf_op jit(solution)/shard_map/ppermute | solution.py:39
  50.4 11.5 %copy-start.3 = (f32[512,512]{1,0:T(8,128)}, f32[512,512]{1,0:T(8,128)S(1)}, u32[]{:S(2)}) copy-start(f32[512,512]{1,0:T(8,128)S(1)} %collective-permute-done.12.b1) | copy-start | bytes 3145732
  50.4 20.8 %collective-permute-start.13 = (f32[512,512]{1,0:T(8,128)}, f32[512,512]{1,0:T(8,128)}, u32[]{:S(2)}, u32[]{:S(2)}) collective-permute-start(f32[512,512]{1,0:T(8,128)} %collective-permute-done.1.a0), channel_id=1, source_target_pairs={{0,72},{1,49},{2,74},{3,51},{4,76},{5,53},{6,78},{7,55},{8,64},{9,... | collective-permute-start | bytes 3145736 | tf_op jit(solution)/shard_map/ppermute | solution.py:39
  55.1 19.0 %collective-permute-start.7 = (f32[512,512]{1,0:T(8,128)}, f32[512,512]{1,0:T(8,128)}, u32[]{:S(2)}, u32[]{:S(2)}) collective-permute-start(f32[512,512]{1,0:T(8,128)} %slice.38), channel_id=1, source_target_pairs={{0,64},{1,17},{2,66},{3,19},{4,68},{5,21},{6,70},{7,23},{8,72},{9,... | collective-permute-start | bytes 3145736 | tf_op jit(solution)/shard_map/ppermute | solution.py:39
  60.9 1.0 copy-start.5
  61.9 15.1 %collective-permute-start.20 = (f32[512,512]{1,0:T(8,128)}, f32[512,512]{1,0:T(8,128)}, u32[]{:S(2)}, u32[]{:S(2)}) collective-permute-start(f32[512,512]{1,0:T(8,128)} %collective-permute-done.6.a1), channel_id=1, source_target_pairs={{0,48},{1,7},{2,50},{3,5},{4,52},{5,3},{6,54},{7,1},{8,56},{9,15},... | collective-permute-start | bytes 3145736 | tf_op jit(solution)/shard_map/ppermute | solution.py:39
  64.4 1.0 copy-start.7
  67.6 15.1 %collective-permute-start.3 = (f32[512,512]{1,0:T(8,128)}, f32[512,512]{1,0:T(8,128)}, u32[]{:S(2)}, u32[]{:S(2)}) collective-permute-start(f32[512,512]{1,0:T(8,128)} %slice.35), channel_id=1, source_target_pairs={{0,16},{1,3},{2,18},{3,1},{4,20},{5,7},{6,22},{7,5},{8,24},{9,11},... | collective-permute-start | bytes 3145736 | tf_op jit(solution)/shard_map/ppermute | solution.py:39
  71.2 20.8 %collective-permute-start.14 = (f32[512,512]{1,0:T(8,128)}, f32[512,512]{1,0:T(8,128)}, u32[]{:S(2)}, u32[]{:S(2)}) collective-permute-start(f32[512,512]{1,0:T(8,128)} %copy-done.7), channel_id=1, source_target_pairs={{0,6},{1,73},{2,4},{3,75},{4,2},{5,77},{6,0},{7,79},{8,14},{9,65},... | collective-permute-start | bytes 3145736 | tf_op jit(solution)/shard_map/ppermute | solution.py:39
  76.4 19.1 %collective-permute-start.8 = (f32[512,512]{1,0:T(8,128)}, f32[512,512]{1,0:T(8,128)}, u32[]{:S(2)}, u32[]{:S(2)}) collective-permute-start(f32[512,512]{1,0:T(8,128)} %slice.39), channel_id=1, source_target_pairs={{0,2},{1,65},{2,0},{3,67},{4,6},{5,69},{6,4},{7,71},{8,10},{9,73},... | collective-permute-start | bytes 3145736 | tf_op jit(solution)/shard_map/ppermute | solution.py:39
  77.0 23.2 %collective-permute-start.21 = (f32[512,512]{1,0:T(8,128)}, f32[512,512]{1,0:T(8,128)}, u32[]{:S(2)}, u32[]{:S(2)}) collective-permute-start(f32[512,512]{1,0:T(8,128)} %collective-permute-done.7.a0), channel_id=1, source_target_pairs={{0,72},{1,49},{2,74},{3,51},{4,76},{5,53},{6,78},{7,55},{8,64},{9,... | collective-permute-start | bytes 3145736 | tf_op jit(solution)/shard_map/ppermute | solution.py:39
  85.0 17.3 %collective-permute-start.4 = (f32[512,512]{1,0:T(8,128)}, f32[512,512]{1,0:T(8,128)}, u32[]{:S(2)}, u32[]{:S(2)}) collective-permute-start(f32[512,512]{1,0:T(8,128)} %slice.36), channel_id=1, source_target_pairs={{0,64},{1,17},{2,66},{3,19},{4,68},{5,21},{6,70},{7,23},{8,72},{9,... | collective-permute-start | bytes 3145736 | tf_op jit(solution)/shard_map/ppermute | solution.py:39
  87.1 1.0 copy-start.9
  88.1 1.0 copy-start.10
  92.0 23.2 %collective-permute-start.15 = (f32[512,512]{1,0:T(8,128)}, f32[512,512]{1,0:T(8,128)S(1)}, u32[]{:S(2)}, u32[]{:S(2)}) collective-permute-start(f32[512,512]{1,0:T(8,128)} %collective-permute-done.3.a1), channel_id=1, source_target_pairs={{0,48},{1,7},{2,50},{3,5},{4,52},{5,3},{6,54},{7,1},{8,56},{9,15},... | collective-permute-start | bytes 3145736 | tf_op jit(solution)/shard_map/ppermute | solution.py:39
  96.8 21.5 %collective-permute-start.9 = (f32[512,512]{1,0:T(8,128)S(1)}, f32[512,512]{1,0:T(8,128)S(1)}, u32[]{:S(2)}, u32[]{:S(2)}) collective-permute-start(f32[512,512]{1,0:T(8,128)S(1)} %slice.40), channel_id=1, source_target_pairs={{0,16},{1,3},{2,18},{3,1},{4,20},{5,7},{6,22},{7,5},{8,24},{9,11},... | collective-permute-start | bytes 3145736 | tf_op jit(solution)/shard_map/ppermute | solution.py:39
  100.2 25.8 %collective-permute-start.22 = (f32[512,512]{1,0:T(8,128)}, f32[512,512]{1,0:T(8,128)S(1)}, u32[]{:S(2)}, u32[]{:S(2)}) collective-permute-start(f32[512,512]{1,0:T(8,128)} %collective-permute-done.8.a2), channel_id=1, source_target_pairs={{0,6},{1,73},{2,4},{3,75},{4,2},{5,77},{6,0},{7,79},{8,14},{9,65},... | collective-permute-start | bytes 3145736 | tf_op jit(solution)/shard_map/ppermute | solution.py:39
  103.6 22.4 %collective-permute-start.10 = (f32[512,512]{1,0:T(8,128)S(1)}, f32[512,512]{1,0:T(8,128)S(1)}, u32[]{:S(2)}, u32[]{:S(2)}) collective-permute-start(f32[512,512]{1,0:T(8,128)S(1)} %slice.41), channel_id=1, source_target_pairs={{0,2},{1,65},{2,0},{3,67},{4,6},{5,69},{6,4},{7,71},{8,10},{9,73},... | collective-permute-start | bytes 3145736 | tf_op jit(solution)/shard_map/ppermute | solution.py:39
  103.9 25.0 %copy-start.16 = (s32[3]{0:T(128)S(1)}, s32[3]{0:T(128)}, u32[]{:S(2)}) copy-start(s32[3]{0:T(128)} %constant.41.clone) | copy-start | bytes 40
  103.9 25.0 %copy-start.17 = (s32[3]{0:T(128)S(1)}, s32[3]{0:T(128)}, u32[]{:S(2)}) copy-start(s32[3]{0:T(128)} %constant.42.clone) | copy-start | bytes 40
  103.9 25.0 %copy-start.2 = (f32[512,512]{1,0:T(8,128)S(1)}, f32[512,512]{1,0:T(8,128)}, u32[]{:S(2)}) copy-start(f32[512,512]{1,0:T(8,128)} %copy-done.1) | copy-start | bytes 3145732
  103.9 25.0 %copy-start.4 = (f32[512,512]{1,0:T(8,128)S(1)}, f32[512,512]{1,0:T(8,128)}, u32[]{:S(2)}) copy-start(f32[512,512]{1,0:T(8,128)} %copy-done.3) | copy-start | bytes 3145732
  103.9 25.0 %copy-start.6 = (f32[512,512]{1,0:T(8,128)S(1)}, f32[512,512]{1,0:T(8,128)}, u32[]{:S(2)}) copy-start(f32[512,512]{1,0:T(8,128)} %copy-done.5) | copy-start | bytes 3145732
  115.2 30.1 %collective-permute-start.16 = (f32[512,512]{1,0:T(8,128)}, f32[512,512]{1,0:T(8,128)S(1)}, u32[]{:S(2)}, u32[]{:S(2)}) collective-permute-start(f32[512,512]{1,0:T(8,128)} %collective-permute-done.4.a0), channel_id=1, source_target_pairs={{0,72},{1,49},{2,74},{3,51},{4,76},{5,53},{6,78},{7,55},{8,64},{9,... | collective-permute-start | bytes 3145736 | tf_op jit(solution)/shard_map/ppermute | solution.py:39
  118.3 27.0 %collective-permute-start.17 = (f32[512,512]{1,0:T(8,128)S(1)}, f32[512,512]{1,0:T(8,128)S(1)}, u32[]{:S(2)}, u32[]{:S(2)}) collective-permute-start(f32[512,512]{1,0:T(8,128)S(1)} %collective-permute-done.9.a1), channel_id=1, source_target_pairs={{0,48},{1,7},{2,50},{3,5},{4,52},{5,3},{6,54},{7,1},{8,56},{9,15},... | collective-permute-start | bytes 3145736 | tf_op jit(solution)/shard_map/ppermute | solution.py:39
  126.0 25.5 %collective-permute-start.23 = (f32[512,512]{1,0:T(8,128)S(1)}, f32[512,512]{1,0:T(8,128)S(1)}, u32[]{:S(2)}, u32[]{:S(2)}) collective-permute-start(f32[512,512]{1,0:T(8,128)S(1)} %collective-permute-done.10.a2), channel_id=1, source_target_pairs={{0,6},{1,73},{2,4},{3,75},{4,2},{5,77},{6,0},{7,79},{8,14},{9,65},... | collective-permute-start | bytes 3145736 | tf_op jit(solution)/shard_map/ppermute | solution.py:39
  129.0 5.1 %copy-start.8 = (f32[512,512]{1,0:T(8,128)S(1)}, f32[512,512]{1,0:T(8,128)}, u32[]{:S(2)}) copy-start(f32[512,512]{1,0:T(8,128)} %copy-done.7) | copy-start | bytes 3145732
where the time goes:
time: 159 us; the launch traced here: 156 us
  waiting for transfers between devices  64.5 us (41%)
  starting transfers between devices  34.9 us (22%)
  Pallas kernels  33.6 us (21%)
  local copies, waits for them, and re-layouts  21.4 us (13%)
  between operations  1.62 us (1%)
    ppermute x25, waiting for transfers between devices, exchange(): return lax.ppermute(x, ('up', 'dn'), pairs)  64.5 us
    ppermute x25, starting transfers between devices, exchange(): return lax.ppermute(x, ('up', 'dn'), pairs)  34.9 us
    pallas_call x4, Pallas kernels, shards(): pl.pallas_call(functools.partial(final_body, i * (size // BLK)), grid=(st...  21.2 us
    slice x10, local copies, waits for them, and re-layouts, shards(): source = lax.slice_in_dim(source, i * size, (i + 1) * size)  16.8 us
    pallas_call x1, Pallas kernels, shards(): pl.pallas_call(local_body, grid=(CHUNKS,), out_shape=jax.ShapeDtypeStruct...  11.2 us
    unnamed x44, local copies, waits for them, and re-layouts  4.1 us
  transfers between devices with their start and end apart: 25, of which 13 were waited for; matrix products, arithmetic and copies ran while one was open for 11% of the time, Pallas kernels for 18%

commit v1 on v0

v1 whole, which is shorter than its diff:
```python
import functools

import jax
import jax.numpy as jnp
from jax import lax
from jax.experimental import pallas as pl
from jax.experimental.pallas import tpu as pltpu
from jax.sharding import PartitionSpec as P

BLK = 128
SIZES = (4, 4, 5, 3)
GAP = 6
ROOM = 32
MASKS = {
    "A": {"x": (4, 0), "y": (1, 0), "z": (0, 2)},
    "B": {"x": (4, 8), "y": (3, 0), "z": (0, 6)},
}
TURN = ("xyz", "yzx")
SMEM = pl.BlockSpec(memory_space=pltpu.SMEM)
F32 = jnp.float32
B16 = jnp.bfloat16


def whole(shape):
    return pl.BlockSpec(shape, lambda *_: (0,) * len(shape))


def params(mib):
    return pltpu.CompilerParams(vmem_limit_bytes=mib << 20)


def exchange(x, mask0, mask1):
    ups, dns = lax.axis_size("up"), lax.axis_size("dn")
    pairs = []
    for u in range(ups):
        for d in range(dns):
            mu, md = (mask0, mask1)[d % 2]
            pairs.append((u * dns + d, (u ^ mu) * dns + (d ^ md)))
    return lax.ppermute(x, ("up", "dn"), pairs)


def halves(x):
    hi = x.astype(B16)
    return hi, (x - hi.astype(F32)).astype(B16)


def thirds(x):
    hi = x.astype(B16).astype(F32)
    mid = (x - hi).astype(B16).astype(F32)
    return hi, mid, (x - hi - mid).astype(B16).astype(F32)


def dot(a, b):
    return jnp.dot(a, b, preferred_element_type=F32)


def slot_of(bits, bit):
    place = jnp.int32(0)
    for k in range(bits.shape[0]):
        place = jnp.where(bits[k] == bit, k, place)
    return place


def column(values):
    row = lax.broadcasted_iota(jnp.int32, (16, BLK), 0)
    out = jnp.zeros((16, BLK), F32)
    for k in range(values.shape[0]):
        out = jnp.where(row == k, values[k], out)
    return out


def prepare(bits_up, bits_dn, signs_dn, site, rep, hop_up, hop_dn, occ_up, occ_dn,
            up_w, loc_w, rem_w, left, right, ou, od):
    dn = lax.axis_index("dn")
    count = loc_w.shape[0] // BLK
    zero = dn % 2 == 0
    for slot in range(8):
        h = hop_up[0] if slot == 0 else hop_up[1 + slot_of(bits_up, slot - 1)]
        hi, lo = halves(h)
        up_w[slot, :BLK, :] = hi
        up_w[slot, BLK:, :] = lo
    loc_w[...] = jnp.zeros_like(loc_w)
    hi, lo = halves(hop_dn[0].T)
    for q in range(4):
        loc_w[q * BLK:(q + 1) * BLK, q * BLK:(q + 1) * BLK] = hi
        loc_w[q * BLK:(q + 1) * BLK, 512 + q * BLK:512 + (q + 1) * BLK] = lo
    for bit in range(2):
        k = slot_of(bits_dn, bit)
        hi, lo = halves(hop_dn[1 + k].T)
        for q in range(4):
            s = signs_dn[k, dn * count + q].astype(F32)
            r = (q ^ (1 << bit)) * BLK
            loc_w[r:r + BLK, q * BLK:(q + 1) * BLK] = (hi.astype(F32) * s).astype(B16)
            loc_w[r:r + BLK, 512 + q * BLK:512 + (q + 1) * BLK] = (lo.astype(F32) * s).astype(B16)
    for t, bit in enumerate((3, jnp.where(zero, 5, 4), jnp.where(zero, 4, 5), 2)):
        k = slot_of(bits_dn, bit)
        hi, lo = halves(hop_dn[1 + k].T)
        for q in range(4):
            s = signs_dn[k, dn * count + q].astype(F32)
            rem_w[q, t * BLK:(t + 1) * BLK, :BLK] = (hi.astype(F32) * s).astype(B16)
            rem_w[q, t * BLK:(t + 1) * BLK, BLK:] = (lo.astype(F32) * s).astype(B16)
    sites = [x[:, :1] for x in thirds(column(site))]
    reps = [x[:, :1] for x in thirds(column(rep))]
    for raw, padded in ((occ_up, ou), (occ_dn, od)):
        padded[...] = jnp.zeros_like(padded)
        padded[:raw.shape[0], :] = raw[...].astype(F32)
    for n in range(3):
        left[16 * n:16 * n + 16, :] = (reps[n] * ou[...]).astype(B16)
        right[16 * n:16 * n + 16, :] = od[...].astype(B16)
        left[48 + 16 * n:64 + 16 * n, :] = (sites[n] * ou[...]).astype(B16)
        right[48 + 16 * n:64 + 16 * n, :] = jnp.ones_like(od).astype(B16)
        left[96 + 16 * n:112 + 16 * n, :] = jnp.ones_like(ou).astype(B16)
        right[96 + 16 * n:112 + 16 * n, :] = (sites[n] * od[...]).astype(B16)


def signed(up_w, slot, s):
    return (up_w[slot].astype(F32) * s).astype(B16)


def local_body(half, firsts, bits_up, signs_up, own, near, far, up_w, loc_w, out, *pieces):
    i = 2 * half + pl.program_id(0)
    first = lax.axis_index("up") * 16 + 4 * i
    places = [slot_of(bits_up, b) for b in range(4)]
    for k, piece in enumerate(pieces):
        low = firsts[k]
        for r in range(low, low + piece.shape[0] // BLK):
            @pl.when(i == r // 4)
            def _(r=r, low=low, piece=piece):
                piece[(r - low) * BLK:(r - low + 1) * BLK, :] = own[r % 4 * BLK:(r % 4 + 1) * BLK, :]

    own_hi, own_lo = halves(own[...])
    near_hi, near_lo = halves(near[...])
    far_hi, far_lo = halves(far[...])
    width = loc_w.shape[0]

    def rows(x, p):
        return x[p * BLK:(p + 1) * BLK]

    across = dot(own_hi, loc_w[...])
    across = across[:, :width] + across[:, width:] + dot(own_lo, loc_w[:, :width])
    for p in range(4):
        w = [up_w[0]] + [
            signed(up_w, 1 + b, signs_up[places[b], first + p].astype(F32)) for b in range(4)
        ]
        w = jnp.concatenate(w, axis=1)

        def stack(o, n, f):
            return jnp.concatenate(
                [rows(o, p), rows(o, p ^ 1), rows(o, p ^ 2), rows(n, p), rows(f, p)], axis=0
            )

        r = dot(w, stack(own_hi, near_hi, far_hi))
        r = r[:BLK] + r[BLK:] + dot(w[:BLK], stack(own_lo, near_lo, far_lo))
        out[p * BLK:(p + 1) * BLK, :] = r + rows(across, p)


def final_body(first, span, bits_up, signs_up, shift, a0, a1, a2, b0, b1, b2, mate, acc, own, up_w, rem_w,
               left, right, *rest):
    residual, updated, mark = rest[-3:]
    zero = lax.axis_index("dn") % 2 == 0
    step = pl.program_id(0)
    slots = (jnp.where(zero, 7, 5), jnp.where(zero, 5, 7), 6)
    places = [slot_of(bits_up, slot - 1) for slot in slots]
    ups = [a0[...], jnp.where(zero, a1[...], a2[...]), jnp.where(zero, b1[...], b0[...])]
    dns = [jnp.where(zero, a2[...], a1[...]), jnp.where(zero, b0[...], b1[...]), b2[...], mate[...]]
    total = acc[...]
    up_parts = [halves(x) for x in ups]
    dn_parts = [halves(x) for x in dns]
    columns = []
    for q in range(4):
        cut = slice(q * BLK, (q + 1) * BLK)
        hi = jnp.concatenate([x[0][:, cut] for x in dn_parts], axis=1)
        lo = jnp.concatenate([x[1][:, cut] for x in dn_parts], axis=1)
        r = dot(hi, rem_w[q])
        columns.append(r[:, :BLK] + r[:, BLK:] + dot(lo, rem_w[q, :, :BLK]))
    total = total + jnp.concatenate(columns, axis=1)
    blocks = []
    for p in range(span // BLK):
        cut = slice(p * BLK, (p + 1) * BLK)
        block = lax.axis_index("up") * 16 + first + step * (span // BLK) + p
        w = jnp.concatenate(
            [signed(up_w, slots[t], signs_up[places[t], block].astype(F32)) for t in range(3)], axis=1
        )
        r = dot(w, jnp.concatenate([x[0][cut] for x in up_parts], axis=0))
        blocks.append(
            r[:BLK] + r[BLK:] + dot(w[:BLK], jnp.concatenate([x[1][cut] for x in up_parts], axis=0))
        )
    total = total + jnp.concatenate(blocks, axis=0)
    gap = lax.dot_general(left[...], right[...], (((0,), (0,)), ((), ())),
                          preferred_element_type=F32) - shift[0]
    c = own[...]
    res = total + gap * c
    residual[...] = res
    updated[...] = c - res / gap
    mark[...] = res[:8, :BLK]


def shards(
    coefficients,
    hopping_up,
    partner_bits_up,
    block_signs_up,
    hopping_down,
    partner_bits_down,
    block_signs_down,
    occupied_up,
    occupied_down,
    site_energy,
    repulsion,
    energy_shift,
):
    rows, width = coefficients.shape
    chunks = len(SIZES)
    starts = [sum(SIZES[:i]) * BLK for i in range(chunks)]
    vmem = pl.BlockSpec(memory_space=pltpu.VMEM)
    up_w, loc_w, rem_w, left, right = pl.pallas_call(
        prepare,
        out_shape=[
            jax.ShapeDtypeStruct((8, 2 * BLK, BLK), B16),
            jax.ShapeDtypeStruct((width, 2 * width), B16),
            jax.ShapeDtypeStruct((4, 4 * BLK, 2 * BLK), B16),
            jax.ShapeDtypeStruct((144, rows), B16),
            jax.ShapeDtypeStruct((144, width), B16),
        ],
        in_specs=[SMEM] * 5 + [vmem] * 4,
        scratch_shapes=[pltpu.VMEM((16, rows), F32), pltpu.VMEM((16, width), F32)],
        compiler_params=params(ROOM),
        cost_estimate=pl.CostEstimate(flops=0, bytes_accessed=4 << 20, transcendentals=0),
        name="prepare",
    )(partner_bits_up, partner_bits_down, block_signs_down, site_energy, repulsion,
      hopping_up, hopping_down, occupied_up, occupied_down)

    block = (4 * BLK, width)
    parts, pieces = [], [lax.slice_in_dim(coefficients, 0, SIZES[0] * BLK)]
    for h in range(2):
        own = [i for i in range(1, chunks) if starts[i] * 2 // rows == h]
        part, *more = pl.pallas_call(
            functools.partial(local_body, h, [starts[i] // BLK for i in own]),
            grid=(2,),
            out_shape=[jax.ShapeDtypeStruct((rows // 2, width), F32)]
            + [jax.ShapeDtypeStruct((SIZES[i] * BLK, width), F32) for i in own],
            in_specs=[
                SMEM,
                SMEM,
                pl.BlockSpec(block, lambda i, h=h: (2 * h + i, 0)),
                pl.BlockSpec(block, lambda i, h=h: ((2 * h + i) ^ 1, 0)),
                pl.BlockSpec(block, lambda i, h=h: ((2 * h + i) ^ 2, 0)),
                whole(up_w.shape),
                whole(loc_w.shape),
            ],
            out_specs=[pl.BlockSpec(block, lambda i: (i, 0))] + [whole((SIZES[i] * BLK, width)) for i in own],
            compiler_params=params(ROOM),
            cost_estimate=pl.CostEstimate(flops=6 << 30, bytes_accessed=12 << 20, transcendentals=0),
            name="local",
        )(partner_bits_up, block_signs_up, coefficients, coefficients, coefficients, up_w, loc_w)
        parts.append(part)
        pieces += more

    def finish(i, outs):
        span = 2 * BLK if (SIZES[i] | starts[i] // BLK) % 2 == 0 else BLK
        tile = (span, width)
        base = starts[i] // span
        here = pl.BlockSpec(tile, lambda s: (s, 0))
        there = pl.BlockSpec(tile, lambda s: (base + s, 0))
        h = starts[i] * 2 // rows
        below = h * rows // 2 // span
        half = pl.BlockSpec(tile, lambda s: (base - below + s, 0))
        arrived = [got[k, j, i] for k in "AB" for j in range(3)]
        operands = [partner_bits_up, block_signs_up, energy_shift.reshape(1), *arrived, got["mate"], got["acc", h], coefficients,
                    up_w, rem_w, left, right]
        tail = [*outs, got["mark"]] if outs else []
        return pl.pallas_call(
            functools.partial(final_body, starts[i] // BLK, span),
            grid=(SIZES[i] * BLK // span,),
            out_shape=[jax.ShapeDtypeStruct((rows, width), F32)] * 2 + [jax.ShapeDtypeStruct((8, BLK), F32)],
            in_specs=[SMEM] * 3 + [here] * 6 + [there, half, there] + [
                whole(up_w.shape),
                whole(rem_w.shape),
                pl.BlockSpec((144, span), lambda s: (0, base + s)),
                whole(right.shape),
            ] + [pl.BlockSpec(memory_space=pl.ANY)] * len(tail),
            out_specs=[there, there, whole((8, BLK))],
            input_output_aliases={len(operands) + k: k for k in range(len(outs))},
            compiler_params=params(ROOM),
            cost_estimate=pl.CostEstimate(flops=3 << 30, bytes_accessed=12 << 20, transcendentals=0),
            name="finish",
        )(*operands, *tail)

    order = [("A", j, 0) for j in range(3)]
    for i in range(chunks):
        for j in range(3):
            order.append(("B", j, i))
            if i + 1 < chunks:
                order.append(("A", j, i + 1))
    got, outs = {}, []
    got["mate"] = exchange(coefficients, (0, 1), (0, 1))
    got["acc", 0], got["acc", 1] = parts
    for n, (kind, j, i) in enumerate(order):
        source = pieces[i] if kind == "A" else got["A", j, i]
        waits = [("acc", 0), "mate"] if n == 3 else []
        if n >= GAP and order[n - GAP][:2] == ("B", 2):
            *outs, got["mark"] = finish(order[n - GAP][2], outs)
            waits = ["mark"]
        if waits:
            source, *held = lax.optimization_barrier((source, *[got[w] for w in waits]))
            got.update(zip(waits, held))
        if kind == "B":
            got["A", j, i] = source
        got[kind, j, i] = exchange(source, MASKS[kind][TURN[0][j]], MASKS[kind][TURN[1][j]])
    for n in range(len(order), len(order) + GAP):
        if order[n - GAP][:2] == ("B", 2):
            *outs, got["mark"] = finish(order[n - GAP][2], outs)
    return tuple(outs)


def solution(mesh):
    placed = (
        P("up", "dn"),
        P(),
        P(),
        P(),
        P(),
        P(),
        P(),
        P(None, "up"),
        P(None, "dn"),
        P(),
        P(),
        P(),
    )
    return jax.shard_map(
        shards,
        mesh=mesh,
        in_specs=placed,
        out_specs=(P("up", "dn"), P("up", "dn")),
        check_vma=False,
    )
```

time: 159 us -> 151 us (0.950); the launches traced: 156 us -> 150 us
  waiting for transfers between devices: 64.5 us -> 48.1 us
  local copies, waits for them, and re-layouts: 21.4 us -> 27.1 us
  starting transfers between devices: 34.9 us -> 38.9 us
    unnamed x44 -> x54, local copies, waits for them, and re-layouts: 4.1 us -> 25.8 us
    ppermute x25, waiting for transfers between devices: 64.5 us -> 48.1 us  [exchange(): return lax.ppermute(x, ('up', 'dn'), pairs)]
    slice x10 -> x1, local copies, waits for them, and re-layouts: 16.8 us -> 1.29 us  [shards(): parts, pieces = ([], [lax.slice_in_dim(coefficients, 0, SIZES[0] * BLK)])]
    ppermute x25, starting transfers between devices: 34.9 us -> 38.9 us  [exchange(): return lax.ppermute(x, ('up', 'dn'), pairs)]
    pallas_call x5 -> x6, Pallas kernels: 32.4 us -> 33.7 us  [the longest x4 21.3 us: finish(): pl.pallas_call(functools.partial(final_body, starts[i] // BLK, span), gri...]
  transfers between devices with their start and end apart: 25 -> 25, of which waited for: 13 -> 7; matrix products, arithmetic and copies ran while one was open for 11% -> 1% of each run, Pallas kernels for 18% -> 21%
where the time goes in v1:
time: 151 us; the launch traced here: 150 us
  waiting for transfers between devices  48.1 us (32%)
  starting transfers between devices  38.9 us (26%)
  Pallas kernels  34.8 us (23%)
  local copies, waits for them, and re-layouts  27.1 us (18%)
    ppermute x25, waiting for transfers between devices, exchange(): return lax.ppermute(x, ('up', 'dn'), pairs)  48.1 us
    ppermute x25, starting transfers between devices, exchange(): return lax.ppermute(x, ('up', 'dn'), pairs)  38.9 us
    unnamed x54, local copies, waits for them, and re-layouts  25.8 us
    pallas_call x4, Pallas kernels, finish(): pl.pallas_call(functools.partial(final_body, starts[i] // BLK, span), gri...  21.3 us
    pallas_call x2, Pallas kernels, shards(): pl.pallas_call(functools.partial(local_body, h, [starts[i] // BLK for i i...  12.4 us
  transfers between devices with their start and end apart: 25, of which 7 were waited for; matrix products, arithmetic and copies ran while one was open for 1% of the time, Pallas kernels for 21%

profile of v1, /device:TPU:16, one launch (start us, length us, event | category | flops | bytes accessed | tf_op | source)
XLA Modules:
  0.0 150.4 jit_solution(2525633656401847991)
XLA Ops:
  0.7 1.3 slice.3
  2.0 1.6 %collective-permute-start.6 = (f32[512,512]{1,0:T(8,128)S(1)}, f32[512,512]{1,0:T(8,128)}, u32[]{:S(2)}, u32[]{:S(2)}) collective-permute-start(f32[512,512]{1,0:T(8,128)S(1)} %slice.3), channel_id=1, source_target_pairs={{0,64},{1,17},{2,66},{3,19},{4,68},{5,21},{6,70},{7,23},{8,72},{9,... | collective-permute-start | bytes 3145736 | tf_op jit(solution)/shard_map/ppermute | solution.py:39
  3.6 1.3 collective-permute-start.14
  4.9 1.9 %collective-permute-start.15 = (f32[512,512]{1,0:T(8,128)S(1)}, f32[512,512]{1,0:T(8,128)}, u32[]{:S(2)}, u32[]{:S(2)}) collective-permute-start(f32[512,512]{1,0:T(8,128)S(1)} %slice.3), channel_id=1, source_target_pairs={{0,2},{1,65},{2,0},{3,67},{4,6},{5,69},{6,4},{7,71},{8,10},{9,73},... | collective-permute-start | bytes 3145736 | tf_op jit(solution)/shard_map/ppermute | solution.py:39
  6.8 1.0 copy-done.13
  7.8 1.0 copy-done.14
  8.9 0.9 copy-done.15
  9.8 0.8 copy-done.18
  11.2 0.7 copy-done.21
  13.8 1.2 prepare.1
  15.0 2.2 %copy-done = f32[2048,512]{1,0:T(8,128)S(1)} copy-done((f32[2048,512]{1,0:T(8,128)S(1)}, f32[2048,512]{1,0:T(8,128)}, u32[]{:S(2)}) %copy-start) | copy-done | bytes 4194328
  17.2 0.7 copy-done.16
  17.9 6.1 %local.3 = (f32[1024,512]{1,0:T(8,128)S(1)}, f32[512,512]{1,0:T(8,128)}) custom-call(s32[7]{0:T(128)S(1)} %copy-done.19, s32[7,128]{1,0:T(8,128)S(1)} %copy-done.16, f32[2048,512]{1,0:T(8,128)S(1)} %copy-done, f32[2048,512]{1,0:T(8,128)S(1)} %copy-done, f32[2048,512]{1,0:T(8,128)S(1)} %copy-done, bf16[8,256,128]{2,1,0:T(8,128)(2,1)S(1)} %get-tuple-element.30.up_w, ...), custom_call_target="tpu_custom_call" | custom-call | flops 6442450944 | bytes 12582912 | tf_op jit(solution)/shard_map/local/pallas_call | solution.py:237
  24.0 1.3 copy-done.5
  26.0 1.8 %collective-permute-start.12 = (f32[512,512]{1,0:T(8,128)}, f32[512,512]{1,0:T(8,128)}, u32[]{:S(2)}, u32[]{:S(2)}) collective-permute-start(f32[512,512]{1,0:T(8,128)} %get-tuple-element.40), channel_id=1, source_target_pairs={{0,16},{1,3},{2,18},{3,1},{4,20},{5,7},{6,22},{7,5},{8,24},{9,11},... | collective-permute-start | bytes 3145736 | tf_op jit(solution)/shard_map/ppermute | solution.py:39
  27.8 0.9 collective-permute-start.17
  28.8 1.0 copy-done.9
  29.7 5.4 %collective-permute-start.18 = (f32[512,512]{1,0:T(8,128)}, f32[512,512]{1,0:T(8,128)}, u32[]{:S(2)}, u32[]{:S(2)}) collective-permute-start(f32[512,512]{1,0:T(8,128)} %collective-permute-done.15.a2), channel_id=1, source_target_pairs={{0,6},{1,73},{2,4},{3,75},{4,2},{5,77},{6,0},{7,79},{8,14},{9,65},... | collective-permute-start | bytes 3145736 | tf_op jit(solution)/shard_map/ppermute | solution.py:39
  35.2 2.0 %copy-done.2 = f32[2048,512]{1,0:T(8,128)} copy-done((f32[2048,512]{1,0:T(8,128)}, f32[2048,512]{1,0:T(8,128)S(1)}, u32[]{:S(2)}) %copy-start.2) | copy-done | bytes 4194328
  37.1 2.1 %collective-permute-start.16 = (f32[512,512]{1,0:T(8,128)}, f32[512,512]{1,0:T(8,128)}, u32[]{:S(2)}, u32[]{:S(2)}) collective-permute-start(f32[512,512]{1,0:T(8,128)} %collective-permute-done.6.a0), channel_id=1, source_target_pairs={{0,72},{1,49},{2,74},{3,51},{4,76},{5,53},{6,78},{7,55},{8,64},{9,... | collective-permute-start | bytes 3145736 | tf_op jit(solution)/shard_map/ppermute | solution.py:39
  39.2 6.3 %local.2 = (f32[1024,512]{1,0:T(8,128)S(1)}, f32[640,512]{1,0:T(8,128)}, f32[384,512]{1,0:T(8,128)S(1)}) custom-call(s32[7]{0:T(128)S(1)} %copy-done.19, s32[7,128]{1,0:T(8,128)S(1)} %copy-done.16, f32[2048,512]{1,0:T(8,128)S(1)} %copy-done, f32[2048,512]{1,0:T(8,128)S(1)} %copy-done, f32[2048,512]{1,0:T(8,128)S(1)} %copy-done, ...), custom_call_target="tpu_custom_call" | custom-call | flops 6442450944 | bytes 12582912 | tf_op jit(solution)/shard_map/local/pallas_call | solution.py:237
  45.5 1.3 copy-done.7
  46.9 0.9 copy-done.25
  48.4 2.0 %collective-permute-done.12.a1 = f32[512,512]{1,0:T(8,128)} collective-permute-done((f32[512,512]{1,0:T(8,128)}, f32[512,512]{1,0:T(8,128)}, u32[]{:S(2)}, u32[]{:S(2)}) %collective-permute-start.12) | collective-permute-done | bytes 1048608 | tf_op jit(solution)/shard_map/ppermute | solution.py:39
  50.3 2.7 %collective-permute-start.13 = (f32[512,512]{1,0:T(8,128)}, f32[512,512]{1,0:T(8,128)}, u32[]{:S(2)}, u32[]{:S(2)}) collective-permute-start(f32[512,512]{1,0:T(8,128)} %get-tuple-element.40), channel_id=1, source_target_pairs={{0,2},{1,65},{2,0},{3,67},{4,6},{5,69},{6,4},{7,71},{8,10},{9,73},... | collective-permute-start | bytes 3145736 | tf_op jit(solution)/shard_map/ppermute | solution.py:39
  53.0 1.0 copy-done.11
  54.0 1.7 %collective-permute-start.9 = (f32[640,512]{1,0:T(8,128)}, f32[640,512]{1,0:T(8,128)}, u32[]{:S(2)}, u32[]{:S(2)}) collective-permute-start(f32[640,512]{1,0:T(8,128)} %get-tuple-element.39), channel_id=1, source_target_pairs={{0,16},{1,3},{2,18},{3,1},{4,20},{5,7},{6,22},{7,5},{8,24},{9,11},... | collective-permute-start | bytes 3932168 | tf_op jit(solution)/shard_map/ppermute | solution.py:39
  56.4 2.8 %collective-permute-start.19 = (f32[512,512]{1,0:T(8,128)S(1)}, f32[512,512]{1,0:T(8,128)S(1)}, u32[]{:S(2)}, u32[]{:S(2)}) collective-permute-start(f32[512,512]{1,0:T(8,128)S(1)} %collective-permute-done.11.a0), channel_id=1, source_target_pairs={{0,72},{1,49},{2,74},{3,51},{4,76},{5,53},{6,78},{7,55},{8,64},{9,... | collective-permute-start | bytes 3145736 | tf_op jit(solution)/shard_map/ppermute | solution.py:39
  59.3 2.2 %copy-done.1 = f32[2048,512]{1,0:T(8,128)S(1)} copy-done((f32[2048,512]{1,0:T(8,128)S(1)}, f32[2048,512]{1,0:T(8,128)}, u32[]{:S(2)}) %copy-start.1) | copy-done | bytes 4194328
  61.5 2.2 %copy-done.3 = f32[2048,512]{1,0:T(8,128)S(1)} copy-done((f32[2048,512]{1,0:T(8,128)S(1)}, f32[2048,512]{1,0:T(8,128)}, u32[]{:S(2)}) %copy-start.3) | copy-done | bytes 4194328
  63.6 1.6 %copy-done.6 = f32[1024,512]{1,0:T(8,128)S(1)} copy-done((f32[1024,512]{1,0:T(8,128)S(1)}, f32[1024,512]{1,0:T(8,128)}, u32[]{:S(2)}) %copy-start.6) | copy-done | bytes 2097176
  65.2 1.2 copy-done.10
  66.5 1.2 copy-done.12
  67.7 5.5 %finish.4 = (f32[2048,512]{1,0:T(8,128)}, f32[2048,512]{1,0:T(8,128)}, f32[8,128]{1,0:T(8,128)S(1)}) custom-call(s32[7]{0:T(128)S(1)} %copy-done.20, s32[7,128]{1,0:T(8,128)S(1)} %copy-done.17, f32[1]{0:T(128)} %bitcast.1.shift, f32[512,512]{1,0:T(8,128)} %collective-permute-done.6.a0, f32[512,512]{1,0:T(8,128)S(1)} %copy-done.10, ...), custom_call_target="tpu_custom_call" | custom-call | flops 3221225472 | bytes 12582912 | tf_op jit(solution)/shard_map/finish/pallas_call | solution.py:272
  73.2 4.2 %collective-permute-done.13.a2 = f32[512,512]{1,0:T(8,128)} collective-permute-done((f32[512,512]{1,0:T(8,128)}, f32[512,512]{1,0:T(8,128)}, u32[]{:S(2)}, u32[]{:S(2)}) %collective-permute-start.13) | collective-permute-done | bytes 1048608 | tf_op jit(solution)/shard_map/ppermute | solution.py:39
  77.4 4.1 %collective-permute-start.21 = (f32[512,512]{1,0:T(8,128)}, f32[512,512]{1,0:T(8,128)S(1)}, u32[]{:S(2)}, u32[]{:S(2)}) collective-permute-start(f32[512,512]{1,0:T(8,128)} %collective-permute-done.13.a2), channel_id=1, source_target_pairs={{0,6},{1,73},{2,4},{3,75},{4,2},{5,77},{6,0},{7,79},{8,14},{9,65},... | collective-permute-start | bytes 3145736 | tf_op jit(solution)/shard_map/ppermute | solution.py:39
  81.4 1.5 %collective-permute-start = (f32[384,512]{1,0:T(8,128)S(1)}, f32[384,512]{1,0:T(8,128)S(1)}, u32[]{:S(2)}, u32[]{:S(2)}) collective-permute-start(f32[384,512]{1,0:T(8,128)S(1)} %copy-done.26), channel_id=1, source_target_pairs={{0,64},{1,17},{2,66},{3,19},{4,68},{5,21},{6,70},{7,23},{8,72},{9,... | collective-permute-start | bytes 2359304 | tf_op jit(solution)/shard_map/ppermute | solution.py:39
  82.9 2.1 %collective-permute-start.22 = (f32[640,512]{1,0:T(8,128)}, f32[640,512]{1,0:T(8,128)S(1)}, u32[]{:S(2)}, u32[]{:S(2)}) collective-permute-start(f32[640,512]{1,0:T(8,128)} %collective-permute-done.8.a0), channel_id=1, source_target_pairs={{0,72},{1,49},{2,74},{3,51},{4,76},{5,53},{6,78},{7,55},{8,64},{9,... | collective-permute-start | bytes 3932168 | tf_op jit(solution)/shard_map/ppermute | solution.py:39
  85.3 20.0 %collective-permute-done.21.b2 = f32[512,512]{1,0:T(8,128)S(1)} collective-permute-done((f32[512,512]{1,0:T(8,128)}, f32[512,512]{1,0:T(8,128)S(1)}, u32[]{:S(2)}, u32[]{:S(2)}) %collective-permute-start.21) | collective-permute-done | bytes 1048608 | tf_op jit(solution)/shard_map/ppermute | solution.py:39
  105.3 5.1 %finish.5 = (f32[2048,512]{1,0:T(8,128)}, f32[2048,512]{1,0:T(8,128)}, f32[8,128]{1,0:T(8,128)S(1)}) custom-call(s32[7]{0:T(128)S(1)} %copy-done.20, s32[7,128]{1,0:T(8,128)S(1)} %copy-done.17, f32[1]{0:T(128)} %bitcast.2.shift, f32[512,512]{1,0:T(8,128)S(1)} %collective-permute-done.11.a0, ...), custom_call_target="tpu_custom_call", output_to_operand_aliasing={{0}: (16, {}), {1}: (17, {})} | custom-call | flops 3221225472 | bytes 12582912 | tf_op jit(solution)/shard_map/finish/pallas_call | solution.py:272
  110.4 3.7 %collective-permute-start.24 = (f32[640,512]{1,0:T(8,128)S(1)}, f32[640,512]{1,0:T(8,128)S(1)}, u32[]{:S(2)}, u32[]{:S(2)}) collective-permute-start(f32[640,512]{1,0:T(8,128)S(1)} %collective-permute-done.10.a2), channel_id=1, source_target_pairs={{0,6},{1,73},{2,4},{3,75},{4,2},{5,77},{6,0},{7,79},{8,14},{9,65},... | collective-permute-start | bytes 3932168 | tf_op jit(solution)/shard_map/ppermute | solution.py:39
  114.0 1.3 collective-permute-start.1
  115.3 10.7 %collective-permute-done.1.a1 = f32[384,512]{1,0:T(8,128)S(1)} collective-permute-done((f32[384,512]{1,0:T(8,128)S(1)}, f32[384,512]{1,0:T(8,128)S(1)}, u32[]{:S(2)}, u32[]{:S(2)}) %collective-permute-start.1) | collective-permute-done | bytes 786464 | tf_op jit(solution)/shard_map/ppermute | solution.py:39
  126.0 2.4 %collective-permute-start.3 = (f32[384,512]{1,0:T(8,128)S(1)}, f32[384,512]{1,0:T(8,128)S(1)}, u32[]{:S(2)}, u32[]{:S(2)}) collective-permute-start(f32[384,512]{1,0:T(8,128)S(1)} %collective-permute-done.a0), channel_id=1, source_target_pairs={{0,72},{1,49},{2,74},{3,51},{4,76},{5,53},{6,78},{7,55},{8,64},{9,... | collective-permute-start | bytes 2359304 | tf_op jit(solution)/shard_map/ppermute | solution.py:39
  128.6 9.5 %collective-permute-done.24.b2 = f32[640,512]{1,0:T(8,128)S(1)} collective-permute-done((f32[640,512]{1,0:T(8,128)S(1)}, f32[640,512]{1,0:T(8,128)S(1)}, u32[]{:S(2)}, u32[]{:S(2)}) %collective-permute-start.24) | collective-permute-done | bytes 1310752 | tf_op jit(solution)/shard_map/ppermute | solution.py:39
  138.1 6.8 %finish.6 = (f32[2048,512]{1,0:T(8,128)}, f32[2048,512]{1,0:T(8,128)}, f32[8,128]{1,0:T(8,128)S(1)}) custom-call(s32[7]{0:T(128)S(1)} %copy-done.20, s32[7,128]{1,0:T(8,128)S(1)} %copy-done.17, f32[1]{0:T(128)} %bitcast.3.shift, f32[640,512]{1,0:T(8,128)} %collective-permute-done.8.a0, ...), custom_call_target="tpu_custom_call", output_to_operand_aliasing={{0}: (16, {}), {1}: (17, {})} | custom-call | flops 3221225472 | bytes 12582912 | tf_op jit(solution)/shard_map/finish/pallas_call | solution.py:272
  144.8 1.6 %collective-permute-done.5.b2 = f32[384,512]{1,0:T(8,128)S(1)} collective-permute-done((f32[384,512]{1,0:T(8,128)S(1)}, f32[384,512]{1,0:T(8,128)S(1)}, u32[]{:S(2)}, u32[]{:S(2)}) %collective-permute-start.5) | collective-permute-done | bytes 786464 | tf_op jit(solution)/shard_map/ppermute | solution.py:39
  146.5 3.9 %finish.7 = (f32[2048,512]{1,0:T(8,128)}, f32[2048,512]{1,0:T(8,128)}, f32[8,128]{1,0:T(8,128)}) custom-call(s32[7]{0:T(128)S(1)} %copy-done.20, s32[7,128]{1,0:T(8,128)S(1)} %copy-done.17, f32[1]{0:T(128)} %bitcast.4.shift, f32[384,512]{1,0:T(8,128)S(1)} %collective-permute-done.a0, ...), custom_call_target="tpu_custom_call", output_to_operand_aliasing={{0}: (16, {}), {1}: (17, {})} | custom-call | flops 3221225472 | bytes 12582912 | tf_op jit(solution)/shard_map/finish/pallas_call | solution.py:272
  (64 shorter events, 4.5 us)
Async XLA Ops:
  0.6 34.5 %collective-permute-start.7 = (f32[2048,512]{1,0:T(8,128)}, f32[2048,512]{1,0:T(8,128)S(1)}, u32[]{:S(2)}, u32[]{:S(2)}) collective-permute-start(f32[2048,512]{1,0:T(8,128)} %own.11), channel_id=1, source_target_pairs={{0,1},{1,0},{2,3},{3,2},{4,5},{5,4},{6,7},{7,6},{8,9},{9,8},{10,11... | collective-permute-start | bytes 12582920 | tf_op jit(solution)/shard_map/ppermute | solution.py:39
  2.0 24.0 %collective-permute-start.6 = (f32[512,512]{1,0:T(8,128)S(1)}, f32[512,512]{1,0:T(8,128)}, u32[]{:S(2)}, u32[]{:S(2)}) collective-permute-start(f32[512,512]{1,0:T(8,128)S(1)} %slice.3), channel_id=1, source_target_pairs={{0,64},{1,17},{2,66},{3,19},{4,68},{5,21},{6,70},{7,23},{8,72},{9,... | collective-permute-start | bytes 3145736 | tf_op jit(solution)/shard_map/ppermute | solution.py:39
  3.6 24.2 %collective-permute-start.14 = (f32[512,512]{1,0:T(8,128)S(1)}, f32[512,512]{1,0:T(8,128)S(1)}, u32[]{:S(2)}, u32[]{:S(2)}) collective-permute-start(f32[512,512]{1,0:T(8,128)S(1)} %slice.3), channel_id=1, source_target_pairs={{0,16},{1,3},{2,18},{3,1},{4,20},{5,7},{6,22},{7,5},{8,24},{9,11},... | collective-permute-start | bytes 3145736 | tf_op jit(solution)/shard_map/ppermute | solution.py:39
  4.9 24.9 %collective-permute-start.15 = (f32[512,512]{1,0:T(8,128)S(1)}, f32[512,512]{1,0:T(8,128)}, u32[]{:S(2)}, u32[]{:S(2)}) collective-permute-start(f32[512,512]{1,0:T(8,128)S(1)} %slice.3), channel_id=1, source_target_pairs={{0,2},{1,65},{2,0},{3,67},{4,6},{5,69},{6,4},{7,71},{8,10},{9,73},... | collective-permute-start | bytes 3145736 | tf_op jit(solution)/shard_map/ppermute | solution.py:39
  6.8 1.0 copy-start.13
  7.8 1.0 copy-start.14
  8.9 0.9 copy-start.15
  9.8 0.8 copy-start.18
  11.2 0.7 copy-start.21
  15.0 2.2 %copy-start = (f32[2048,512]{1,0:T(8,128)S(1)}, f32[2048,512]{1,0:T(8,128)}, u32[]{:S(2)}) copy-start(f32[2048,512]{1,0:T(8,128)} %own.11) | copy-start | bytes 12582916
  17.2 0.7 copy-start.16
  24.0 1.3 copy-start.5
  25.3 22.4 %collective-permute-start.11 = (f32[512,512]{1,0:T(8,128)}, f32[512,512]{1,0:T(8,128)S(1)}, u32[]{:S(2)}, u32[]{:S(2)}) collective-permute-start(f32[512,512]{1,0:T(8,128)} %get-tuple-element.40), channel_id=1, source_target_pairs={{0,64},{1,17},{2,66},{3,19},{4,68},{5,21},{6,70},{7,23},{8,72},{9,... | collective-permute-start | bytes 3145736 | tf_op jit(solution)/shard_map/ppermute | solution.py:39
  26.0 24.3 %collective-permute-start.12 = (f32[512,512]{1,0:T(8,128)}, f32[512,512]{1,0:T(8,128)}, u32[]{:S(2)}, u32[]{:S(2)}) collective-permute-start(f32[512,512]{1,0:T(8,128)} %get-tuple-element.40), channel_id=1, source_target_pairs={{0,16},{1,3},{2,18},{3,1},{4,20},{5,7},{6,22},{7,5},{8,24},{9,11},... | collective-permute-start | bytes 3145736 | tf_op jit(solution)/shard_map/ppermute | solution.py:39
  27.8 25.2 %collective-permute-start.17 = (f32[512,512]{1,0:T(8,128)S(1)}, f32[512,512]{1,0:T(8,128)S(1)}, u32[]{:S(2)}, u32[]{:S(2)}) collective-permute-start(f32[512,512]{1,0:T(8,128)S(1)} %collective-permute-done.14.a1), channel_id=1, source_target_pairs={{0,48},{1,7},{2,50},{3,5},{4,52},{5,3},{6,54},{7,1},{8,56},{9,15},... | collective-permute-start | bytes 3145736 | tf_op jit(solution)/shard_map/ppermute | solution.py:39
  28.8 1.0 copy-start.9
  29.7 26.7 %collective-permute-start.18 = (f32[512,512]{1,0:T(8,128)}, f32[512,512]{1,0:T(8,128)}, u32[]{:S(2)}, u32[]{:S(2)}) collective-permute-start(f32[512,512]{1,0:T(8,128)} %collective-permute-done.15.a2), channel_id=1, source_target_pairs={{0,6},{1,73},{2,4},{3,75},{4,2},{5,77},{6,0},{7,79},{8,14},{9,65},... | collective-permute-start | bytes 3145736 | tf_op jit(solution)/shard_map/ppermute | solution.py:39
  35.2 2.0 %copy-start.2 = (f32[2048,512]{1,0:T(8,128)}, f32[2048,512]{1,0:T(8,128)S(1)}, u32[]{:S(2)}) copy-start(f32[2048,512]{1,0:T(8,128)S(1)} %collective-permute-done.7.mate) | copy-start | bytes 12582916
  37.1 22.1 %copy-start.17 = (s32[7,128]{1,0:T(8,128)S(1)}, s32[7,128]{1,0:T(8,128)}, u32[]{:S(2)}) copy-start(s32[7,128]{1,0:T(8,128)} %signs_up.11) | copy-start | bytes 10756
  37.1 22.1 %copy-start.20 = (s32[7]{0:T(128)S(1)}, s32[7]{0:T(128)}, u32[]{:S(2)}) copy-start(s32[7]{0:T(128)} %bits_up.13) | copy-start | bytes 88
  37.1 22.1 %collective-permute-start.16 = (f32[512,512]{1,0:T(8,128)}, f32[512,512]{1,0:T(8,128)}, u32[]{:S(2)}, u32[]{:S(2)}) collective-permute-start(f32[512,512]{1,0:T(8,128)} %collective-permute-done.6.a0), channel_id=1, source_target_pairs={{0,72},{1,49},{2,74},{3,51},{4,76},{5,53},{6,78},{7,55},{8,64},{9,... | collective-permute-start | bytes 3145736 | tf_op jit(solution)/shard_map/ppermute | solution.py:39
  45.5 1.3 copy-start.7
  46.9 0.9 copy-start.25
  47.8 33.7 %collective-permute-start.8 = (f32[640,512]{1,0:T(8,128)}, f32[640,512]{1,0:T(8,128)}, u32[]{:S(2)}, u32[]{:S(2)}) collective-permute-start(f32[640,512]{1,0:T(8,128)} %get-tuple-element.39), channel_id=1, source_target_pairs={{0,64},{1,17},{2,66},{3,19},{4,68},{5,21},{6,70},{7,23},{8,72},{9,... | collective-permute-start | bytes 3932168 | tf_op jit(solution)/shard_map/ppermute | solution.py:39
  50.3 27.0 %collective-permute-start.13 = (f32[512,512]{1,0:T(8,128)}, f32[512,512]{1,0:T(8,128)}, u32[]{:S(2)}, u32[]{:S(2)}) collective-permute-start(f32[512,512]{1,0:T(8,128)} %get-tuple-element.40), channel_id=1, source_target_pairs={{0,2},{1,65},{2,0},{3,67},{4,6},{5,69},{6,4},{7,71},{8,10},{9,73},... | collective-permute-start | bytes 3145736 | tf_op jit(solution)/shard_map/ppermute | solution.py:39
  53.0 1.0 copy-start.11
  54.0 27.4 %collective-permute-start.9 = (f32[640,512]{1,0:T(8,128)}, f32[640,512]{1,0:T(8,128)}, u32[]{:S(2)}, u32[]{:S(2)}) collective-permute-start(f32[640,512]{1,0:T(8,128)} %get-tuple-element.39), channel_id=1, source_target_pairs={{0,16},{1,3},{2,18},{3,1},{4,20},{5,7},{6,22},{7,5},{8,24},{9,11},... | collective-permute-start | bytes 3932168 | tf_op jit(solution)/shard_map/ppermute | solution.py:39
  56.4 26.5 %collective-permute-start.19 = (f32[512,512]{1,0:T(8,128)S(1)}, f32[512,512]{1,0:T(8,128)S(1)}, u32[]{:S(2)}, u32[]{:S(2)}) collective-permute-start(f32[512,512]{1,0:T(8,128)S(1)} %collective-permute-done.11.a0), channel_id=1, source_target_pairs={{0,72},{1,49},{2,74},{3,51},{4,76},{5,53},{6,78},{7,55},{8,64},{9,... | collective-permute-start | bytes 3145736 | tf_op jit(solution)/shard_map/ppermute | solution.py:39
  59.2 25.8 %collective-permute-start.20 = (f32[512,512]{1,0:T(8,128)}, f32[512,512]{1,0:T(8,128)S(1)}, u32[]{:S(2)}, u32[]{:S(2)}) collective-permute-start(f32[512,512]{1,0:T(8,128)} %collective-permute-done.12.a1), channel_id=1, source_target_pairs={{0,48},{1,7},{2,50},{3,5},{4,52},{5,3},{6,54},{7,1},{8,56},{9,15},... | collective-permute-start | bytes 3145736 | tf_op jit(solution)/shard_map/ppermute | solution.py:39
  59.3 2.2 %copy-start.1 = (f32[2048,512]{1,0:T(8,128)S(1)}, f32[2048,512]{1,0:T(8,128)}, u32[]{:S(2)}) copy-start(f32[2048,512]{1,0:T(8,128)} %own.11) | copy-start | bytes 12582916
  61.5 2.2 %copy-start.3 = (f32[2048,512]{1,0:T(8,128)S(1)}, f32[2048,512]{1,0:T(8,128)}, u32[]{:S(2)}) copy-start(f32[2048,512]{1,0:T(8,128)} %copy-done.2) | copy-start | bytes 12582916
  63.6 1.6 %copy-start.6 = (f32[1024,512]{1,0:T(8,128)S(1)}, f32[1024,512]{1,0:T(8,128)}, u32[]{:S(2)}) copy-start(f32[1024,512]{1,0:T(8,128)} %copy-done.5) | copy-start | bytes 6291460
  65.2 1.2 copy-start.10
  66.5 1.2 copy-start.12
  67.7 13.7 %copy-start.26 = (f32[384,512]{1,0:T(8,128)S(1)}, f32[384,512]{1,0:T(8,128)}, u32[]{:S(2)}) copy-start(f32[384,512]{1,0:T(8,128)} %copy-done.25) | copy-start | bytes 2359300
  67.7 37.6 %copy-start.4 = (f32[2048,512]{1,0:T(8,128)S(1)}, f32[2048,512]{1,0:T(8,128)}, u32[]{:S(2)}) copy-start(f32[2048,512]{1,0:T(8,128)} %copy-done.2) | copy-start | bytes 12582916
  77.4 27.9 %collective-permute-start.21 = (f32[512,512]{1,0:T(8,128)}, f32[512,512]{1,0:T(8,128)S(1)}, u32[]{:S(2)}, u32[]{:S(2)}) collective-permute-start(f32[512,512]{1,0:T(8,128)} %collective-permute-done.13.a2), channel_id=1, source_target_pairs={{0,6},{1,73},{2,4},{3,75},{4,2},{5,77},{6,0},{7,79},{8,14},{9,65},... | collective-permute-start | bytes 3145736 | tf_op jit(solution)/shard_map/ppermute | solution.py:39
  81.4 29.0 %collective-permute-start.10 = (f32[640,512]{1,0:T(8,128)}, f32[640,512]{1,0:T(8,128)S(1)}, u32[]{:S(2)}, u32[]{:S(2)}) collective-permute-start(f32[640,512]{1,0:T(8,128)} %get-tuple-element.39), channel_id=1, source_target_pairs={{0,2},{1,65},{2,0},{3,67},{4,6},{5,69},{6,4},{7,71},{8,10},{9,73},... | collective-permute-start | bytes 3932168 | tf_op jit(solution)/shard_map/ppermute | solution.py:39
  81.4 33.9 %collective-permute-start = (f32[384,512]{1,0:T(8,128)S(1)}, f32[384,512]{1,0:T(8,128)S(1)}, u32[]{:S(2)}, u32[]{:S(2)}) collective-permute-start(f32[384,512]{1,0:T(8,128)S(1)} %copy-done.26), channel_id=1, source_target_pairs={{0,64},{1,17},{2,66},{3,19},{4,68},{5,21},{6,70},{7,23},{8,72},{9,... | collective-permute-start | bytes 2359304 | tf_op jit(solution)/shard_map/ppermute | solution.py:39
  82.9 45.5 %collective-permute-start.22 = (f32[640,512]{1,0:T(8,128)}, f32[640,512]{1,0:T(8,128)S(1)}, u32[]{:S(2)}, u32[]{:S(2)}) collective-permute-start(f32[640,512]{1,0:T(8,128)} %collective-permute-done.8.a0), channel_id=1, source_target_pairs={{0,72},{1,49},{2,74},{3,51},{4,76},{5,53},{6,78},{7,55},{8,64},{9,... | collective-permute-start | bytes 3932168 | tf_op jit(solution)/shard_map/ppermute | solution.py:39
  85.0 43.6 %collective-permute-start.23 = (f32[640,512]{1,0:T(8,128)}, f32[640,512]{1,0:T(8,128)S(1)}, u32[]{:S(2)}, u32[]{:S(2)}) collective-permute-start(f32[640,512]{1,0:T(8,128)} %collective-permute-done.9.a1), channel_id=1, source_target_pairs={{0,48},{1,7},{2,50},{3,5},{4,52},{5,3},{6,54},{7,1},{8,56},{9,15},... | collective-permute-start | bytes 3932168 | tf_op jit(solution)/shard_map/ppermute | solution.py:39
  105.3 32.8 %copy-start.8 = (f32[1024,512]{1,0:T(8,128)S(1)}, f32[1024,512]{1,0:T(8,128)}, u32[]{:S(2)}) copy-start(f32[1024,512]{1,0:T(8,128)} %copy-done.7) | copy-start | bytes 6291460
  110.4 27.7 %collective-permute-start.24 = (f32[640,512]{1,0:T(8,128)S(1)}, f32[640,512]{1,0:T(8,128)S(1)}, u32[]{:S(2)}, u32[]{:S(2)}) collective-permute-start(f32[640,512]{1,0:T(8,128)S(1)} %collective-permute-done.10.a2), channel_id=1, source_target_pairs={{0,6},{1,73},{2,4},{3,75},{4,2},{5,77},{6,0},{7,79},{8,14},{9,65},... | collective-permute-start | bytes 3932168 | tf_op jit(solution)/shard_map/ppermute | solution.py:39
  114.0 12.0 %collective-permute-start.1 = (f32[384,512]{1,0:T(8,128)S(1)}, f32[384,512]{1,0:T(8,128)S(1)}, u32[]{:S(2)}, u32[]{:S(2)}) collective-permute-start(f32[384,512]{1,0:T(8,128)S(1)} %copy-done.26), channel_id=1, source_target_pairs={{0,16},{1,3},{2,18},{3,1},{4,20},{5,7},{6,22},{7,5},{8,24},{9,11},... | collective-permute-start | bytes 2359304 | tf_op jit(solution)/shard_map/ppermute | solution.py:39
  115.3 13.1 %collective-permute-start.2 = (f32[384,512]{1,0:T(8,128)S(1)}, f32[384,512]{1,0:T(8,128)S(1)}, u32[]{:S(2)}, u32[]{:S(2)}) collective-permute-start(f32[384,512]{1,0:T(8,128)S(1)} %copy-done.26), channel_id=1, source_target_pairs={{0,2},{1,65},{2,0},{3,67},{4,6},{5,69},{6,4},{7,71},{8,10},{9,73},... | collective-permute-start | bytes 2359304 | tf_op jit(solution)/shard_map/ppermute | solution.py:39
  126.0 18.8 %collective-permute-start.3 = (f32[384,512]{1,0:T(8,128)S(1)}, f32[384,512]{1,0:T(8,128)S(1)}, u32[]{:S(2)}, u32[]{:S(2)}) collective-permute-start(f32[384,512]{1,0:T(8,128)S(1)} %collective-permute-done.a0), channel_id=1, source_target_pairs={{0,72},{1,49},{2,74},{3,51},{4,76},{5,53},{6,78},{7,55},{8,64},{9,... | collective-permute-start | bytes 2359304 | tf_op jit(solution)/shard_map/ppermute | solution.py:39
  128.4 16.4 %collective-permute-start.4 = (f32[384,512]{1,0:T(8,128)S(1)}, f32[384,512]{1,0:T(8,128)S(1)}, u32[]{:S(2)}, u32[]{:S(2)}) collective-permute-start(f32[384,512]{1,0:T(8,128)S(1)} %collective-permute-done.1.a1), channel_id=1, source_target_pairs={{0,48},{1,7},{2,50},{3,5},{4,52},{5,3},{6,54},{7,1},{8,56},{9,15},... | collective-permute-start | bytes 2359304 | tf_op jit(solution)/shard_map/ppermute | solution.py:39
  128.4 18.1 %collective-permute-start.5 = (f32[384,512]{1,0:T(8,128)S(1)}, f32[384,512]{1,0:T(8,128)S(1)}, u32[]{:S(2)}, u32[]{:S(2)}) collective-permute-start(f32[384,512]{1,0:T(8,128)S(1)} %collective-permute-done.2.a2), channel_id=1, source_target_pairs={{0,6},{1,73},{2,4},{3,75},{4,2},{5,77},{6,0},{7,79},{8,14},{9,65},... | collective-permute-start | bytes 2359304 | tf_op jit(solution)/shard_map/ppermute | solution.py:39
  (4 other events, 2.6 us)

commit v2 on v1

--- a/solution.py
+++ b/solution.py
@@ -10,6 +10,7 @@
 BLK = 128
 SIZES = (4, 4, 5, 3)
 GAP = 6
+EARLY = (3,)
 ROOM = 32
 MASKS = {
     "A": {"x": (4, 0), "y": (1, 0), "z": (0, 2)},
@@ -195,6 +196,65 @@
     mark[...] = res[:8, :BLK]
 
 
+def remote(first, span, bits_up, signs_up, slots, ups, dns, up_w, weight):
+    step = pl.program_id(0)
+    places = [slot_of(bits_up, slot - 1) for slot in slots]
+    up_parts = [halves(x) for x in ups]
+    dn_parts = [halves(x) for x in dns]
+    columns = []
+    for q in range(4):
+        cut = slice(q * BLK, (q + 1) * BLK)
+        hi = jnp.concatenate([x[0][:, cut] for x in dn_parts], axis=1)
+        lo = jnp.concatenate([x[1][:, cut] for x in dn_parts], axis=1)
+        r = dot(hi, weight(q))
+        columns.append(r[:, :BLK] + r[:, BLK:] + dot(lo, weight(q)[:, :BLK]))
+    total = jnp.concatenate(columns, axis=1)
+    blocks = []
+    for p in range(span // BLK):
+        cut = slice(p * BLK, (p + 1) * BLK)
+        block = lax.axis_index("up") * 16 + first + step * (span // BLK) + p
+        w = jnp.concatenate(
+            [signed(up_w, slots[t], signs_up[places[t], block].astype(F32)) for t in range(len(slots))], axis=1
+        )
+        r = dot(w, jnp.concatenate([x[0][cut] for x in up_parts], axis=0))
+        blocks.append(
+            r[:BLK] + r[BLK:] + dot(w[:BLK], jnp.concatenate([x[1][cut] for x in up_parts], axis=0))
+        )
+    return total + jnp.concatenate(blocks, axis=0)
+
+
+def early_body(first, span, bits_up, signs_up, a0, a1, a2, mate, acc, up_w, rem_w, out):
+    zero = lax.axis_index("dn") % 2 == 0
+    slots = (jnp.where(zero, 7, 5), jnp.where(zero, 5, 7))
+    ups = [a0[...], jnp.where(zero, a1[...], a2[...])]
+    dns = [jnp.where(zero, a2[...], a1[...]), mate[...]]
+
+    def weight(q):
+        return jnp.concatenate([rem_w[q, :BLK], rem_w[q, 3 * BLK:]], axis=0)
+
+    out[...] = acc[...] + remote(first, span, bits_up, signs_up, slots, ups, dns, up_w, weight)
+
+
+def late_body(first, span, bits_up, signs_up, shift, b0, b1, b2, acc, own, up_w, rem_w,
+               left, right, *rest):
+    residual, updated, mark = rest[-3:]
+    zero = lax.axis_index("dn") % 2 == 0
+    ups = [jnp.where(zero, b1[...], b0[...])]
+    dns = [jnp.where(zero, b0[...], b1[...]), b2[...]]
+
+    def weight(q):
+        return rem_w[q, BLK:3 * BLK]
+
+    total = acc[...] + remote(first, span, bits_up, signs_up, (6,), ups, dns, up_w, weight)
+    gap = lax.dot_general(left[...], right[...], (((0,), (0,)), ((), ())),
+                          preferred_element_type=F32) - shift[0]
+    c = own[...]
+    res = total + gap * c
+    residual[...] = res
+    updated[...] = c - res / gap
+    mark[...] = res[:8, :BLK]
+
+
 def shards(
     coefficients,
     hopping_up,
@@ -269,11 +329,27 @@
         operands = [partner_bits_up, block_signs_up, energy_shift.reshape(1), *arrived, got["mate"], got["acc", h], coefficients,
                     up_w, rem_w, left, right]
         tail = [*outs, got["mark"]] if outs else []
+        body = final_body
+        near = [here] * 6 + [there, half, there]
+        if i in EARLY:
+            sofar = pl.pallas_call(
+                functools.partial(early_body, starts[i] // BLK, span),
+                grid=(SIZES[i] * BLK // span,),
+                out_shape=jax.ShapeDtypeStruct((SIZES[i] * BLK, width), F32),
+                in_specs=[SMEM] * 2 + [here] * 3 + [there, half, whole(up_w.shape), whole(rem_w.shape)],
+                out_specs=here,
+                compiler_params=params(ROOM),
+                cost_estimate=pl.CostEstimate(flops=2 << 30, bytes_accessed=8 << 20, transcendentals=0),
+                name="early",
+            )(*operands[:2], *arrived[:3], got["mate"], got["acc", h], up_w, rem_w)
+            operands[3:11] = [*arrived[3:], sofar]
+            body = late_body
+            near = [here] * 4 + [there]
         return pl.pallas_call(
-            functools.partial(final_body, starts[i] // BLK, span),
+            functools.partial(body, starts[i] // BLK, span),
             grid=(SIZES[i] * BLK // span,),
             out_shape=[jax.ShapeDtypeStruct((rows, width), F32)] * 2 + [jax.ShapeDtypeStruct((8, BLK), F32)],
-            in_specs=[SMEM] * 3 + [here] * 6 + [there, half, there] + [
+            in_specs=[SMEM] * 3 + near + [
                 whole(up_w.shape),
                 whole(rem_w.shape),
                 pl.BlockSpec((144, span), lambda s: (0, base + s)),

time: 151 us -> 151 us (level)
  waiting for transfers between devices: 48.1 us -> 41.3 us
  local copies, waits for them, and re-layouts: 27.1 us -> 30.4 us
  Pallas kernels: 34.8 us -> 37.7 us
    ppermute x25, waiting for transfers between devices: 48.1 us -> 41.3 us  [exchange(): return lax.ppermute(x, ('up', 'dn'), pairs)]
    unnamed x54 -> x62, local copies, waits for them, and re-layouts: 25.8 us -> 29.1 us
    pallas_call x4 -> x5, Pallas kernels: 21.3 us -> 24.1 us  [the longest x4 20.7 us: finish(): pl.pallas_call(functools.partial(body, starts[i] // BLK, span), grid=(SIZ...]
  transfers between devices with their start and end apart: 25 -> 25, of which waited for: 7 -> 7; matrix products, arithmetic and copies ran while one was open for 1% -> 1% of each run, Pallas kernels for 21% -> 23%
where the time goes in v2:
time: 151 us; the launch traced here: 150 us
  waiting for transfers between devices  41.3 us (27%)
  starting transfers between devices  38.8 us (26%)
  Pallas kernels  37.7 us (25%)
  local copies, waits for them, and re-layouts  30.4 us (20%)
    ppermute x25, waiting for transfers between devices, exchange(): return lax.ppermute(x, ('up', 'dn'), pairs)  41.3 us
    ppermute x25, starting transfers between devices, exchange(): return lax.ppermute(x, ('up', 'dn'), pairs)  38.8 us
    unnamed x62, local copies, waits for them, and re-layouts  29.1 us
    pallas_call x4, Pallas kernels, finish(): pl.pallas_call(functools.partial(body, starts[i] // BLK, span), grid=(SIZ...  20.7 us
    pallas_call x2, Pallas kernels, shards(): pl.pallas_call(functools.partial(local_body, h, [starts[i] // BLK for i i...  12.4 us
    pallas_call x1, Pallas kernels, finish(): pl.pallas_call(functools.partial(early_body, starts[i] // BLK, span), gri...  3.49 us
  transfers between devices with their start and end apart: 25, of which 7 were waited for; matrix products, arithmetic and copies ran while one was open for 1% of the time, Pallas kernels for 23%

profile of v2, /device:TPU:16, one launch (start us, length us, event | category | flops | bytes accessed | tf_op | source)
XLA Modules:
  0.0 149.7 jit_solution(9682678415453528184)
XLA Ops:
  0.7 1.3 slice.3
  2.0 1.6 %collective-permute-start.6 = (f32[512,512]{1,0:T(8,128)S(1)}, f32[512,512]{1,0:T(8,128)}, u32[]{:S(2)}, u32[]{:S(2)}) collective-permute-start(f32[512,512]{1,0:T(8,128)S(1)} %slice.3), channel_id=1, source_target_pairs={{0,64},{1,17},{2,66},{3,19},{4,68},{5,21},{6,70},{7,23},{8,72},{9,... | collective-permute-start | bytes 3145736 | tf_op jit(solution)/shard_map/ppermute | solution.py:40
  3.6 1.3 collective-permute-start.14
  4.9 1.9 %collective-permute-start.15 = (f32[512,512]{1,0:T(8,128)S(1)}, f32[512,512]{1,0:T(8,128)}, u32[]{:S(2)}, u32[]{:S(2)}) collective-permute-start(f32[512,512]{1,0:T(8,128)S(1)} %slice.3), channel_id=1, source_target_pairs={{0,2},{1,65},{2,0},{3,67},{4,6},{5,69},{6,4},{7,71},{8,10},{9,73},... | collective-permute-start | bytes 3145736 | tf_op jit(solution)/shard_map/ppermute | solution.py:40
  6.8 1.0 copy-done.17
  7.8 1.0 copy-done.18
  8.9 0.9 copy-done.19
  9.8 0.8 copy-done.22
  13.8 1.2 prepare.1
  15.0 2.2 %copy-done = f32[2048,512]{1,0:T(8,128)S(1)} copy-done((f32[2048,512]{1,0:T(8,128)S(1)}, f32[2048,512]{1,0:T(8,128)}, u32[]{:S(2)}) %copy-start) | copy-done | bytes 4194328
  17.9 6.1 %local.3 = (f32[1024,512]{1,0:T(8,128)S(1)}, f32[512,512]{1,0:T(8,128)}) custom-call(s32[7]{0:T(128)S(1)} %copy-done.23, s32[7,128]{1,0:T(8,128)S(1)} %copy-done.20, f32[2048,512]{1,0:T(8,128)S(1)} %copy-done, f32[2048,512]{1,0:T(8,128)S(1)} %copy-done, f32[2048,512]{1,0:T(8,128)S(1)} %copy-done, bf16[8,256,128]{2,1,0:T(8,128)(2,1)S(1)} %get-tuple-element.30.up_w, ...), custom_call_target="tpu_custom_call" | custom-call | flops 6442450944 | bytes 12582912 | tf_op jit(solution)/shard_map/local/pallas_call | solution.py:297
  24.0 1.3 copy-done.9
  26.0 1.8 %collective-permute-start.12 = (f32[512,512]{1,0:T(8,128)}, f32[512,512]{1,0:T(8,128)}, u32[]{:S(2)}, u32[]{:S(2)}) collective-permute-start(f32[512,512]{1,0:T(8,128)} %get-tuple-element.40), channel_id=1, source_target_pairs={{0,16},{1,3},{2,18},{3,1},{4,20},{5,7},{6,22},{7,5},{8,24},{9,11},... | collective-permute-start | bytes 3145736 | tf_op jit(solution)/shard_map/ppermute | solution.py:40
  27.8 0.9 collective-permute-start.17
  28.7 1.0 copy-done.13
  29.7 5.4 %collective-permute-start.18 = (f32[512,512]{1,0:T(8,128)}, f32[512,512]{1,0:T(8,128)}, u32[]{:S(2)}, u32[]{:S(2)}) collective-permute-start(f32[512,512]{1,0:T(8,128)} %collective-permute-done.15.a2), channel_id=1, source_target_pairs={{0,6},{1,73},{2,4},{3,75},{4,2},{5,77},{6,0},{7,79},{8,14},{9,65},... | collective-permute-start | bytes 3145736 | tf_op jit(solution)/shard_map/ppermute | solution.py:40
  35.2 2.0 %copy-done.3 = f32[2048,512]{1,0:T(8,128)} copy-done((f32[2048,512]{1,0:T(8,128)}, f32[2048,512]{1,0:T(8,128)S(1)}, u32[]{:S(2)}) %copy-start.3) | copy-done | bytes 4194328
  37.2 2.1 %collective-permute-start.16 = (f32[512,512]{1,0:T(8,128)}, f32[512,512]{1,0:T(8,128)}, u32[]{:S(2)}, u32[]{:S(2)}) collective-permute-start(f32[512,512]{1,0:T(8,128)} %collective-permute-done.6.a0), channel_id=1, source_target_pairs={{0,72},{1,49},{2,74},{3,51},{4,76},{5,53},{6,78},{7,55},{8,64},{9,... | collective-permute-start | bytes 3145736 | tf_op jit(solution)/shard_map/ppermute | solution.py:40
  39.2 6.3 %local.2 = (f32[1024,512]{1,0:T(8,128)S(1)}, f32[640,512]{1,0:T(8,128)}, f32[384,512]{1,0:T(8,128)S(1)}) custom-call(s32[7]{0:T(128)S(1)} %copy-done.23, s32[7,128]{1,0:T(8,128)S(1)} %copy-done.20, f32[2048,512]{1,0:T(8,128)S(1)} %copy-done, f32[2048,512]{1,0:T(8,128)S(1)} %copy-done, f32[2048,512]{1,0:T(8,128)S(1)} %copy-done, ...), custom_call_target="tpu_custom_call" | custom-call | flops 6442450944 | bytes 12582912 | tf_op jit(solution)/shard_map/local/pallas_call | solution.py:297
  45.5 1.4 copy-done.6
  46.9 0.9 copy-done.29
  48.4 2.0 %collective-permute-done.12.a1 = f32[512,512]{1,0:T(8,128)} collective-permute-done((f32[512,512]{1,0:T(8,128)}, f32[512,512]{1,0:T(8,128)}, u32[]{:S(2)}, u32[]{:S(2)}) %collective-permute-start.12) | collective-permute-done | bytes 1048608 | tf_op jit(solution)/shard_map/ppermute | solution.py:40
  50.4 2.7 %collective-permute-start.13 = (f32[512,512]{1,0:T(8,128)}, f32[512,512]{1,0:T(8,128)}, u32[]{:S(2)}, u32[]{:S(2)}) collective-permute-start(f32[512,512]{1,0:T(8,128)} %get-tuple-element.40), channel_id=1, source_target_pairs={{0,2},{1,65},{2,0},{3,67},{4,6},{5,69},{6,4},{7,71},{8,10},{9,73},... | collective-permute-start | bytes 3145736 | tf_op jit(solution)/shard_map/ppermute | solution.py:40
  53.0 1.0 copy-done.15
  54.0 1.7 %collective-permute-start.9 = (f32[640,512]{1,0:T(8,128)}, f32[640,512]{1,0:T(8,128)}, u32[]{:S(2)}, u32[]{:S(2)}) collective-permute-start(f32[640,512]{1,0:T(8,128)} %get-tuple-element.39), channel_id=1, source_target_pairs={{0,16},{1,3},{2,18},{3,1},{4,20},{5,7},{6,22},{7,5},{8,24},{9,11},... | collective-permute-start | bytes 3932168 | tf_op jit(solution)/shard_map/ppermute | solution.py:40
  56.4 2.8 %collective-permute-start.19 = (f32[512,512]{1,0:T(8,128)S(1)}, f32[512,512]{1,0:T(8,128)S(1)}, u32[]{:S(2)}, u32[]{:S(2)}) collective-permute-start(f32[512,512]{1,0:T(8,128)S(1)} %collective-permute-done.11.a0), channel_id=1, source_target_pairs={{0,72},{1,49},{2,74},{3,51},{4,76},{5,53},{6,78},{7,55},{8,64},{9,... | collective-permute-start | bytes 3145736 | tf_op jit(solution)/shard_map/ppermute | solution.py:40
  59.3 2.2 %copy-done.1 = f32[2048,512]{1,0:T(8,128)S(1)} copy-done((f32[2048,512]{1,0:T(8,128)S(1)}, f32[2048,512]{1,0:T(8,128)}, u32[]{:S(2)}) %copy-start.1) | copy-done | bytes 4194328
  61.5 2.2 %copy-done.4 = f32[2048,512]{1,0:T(8,128)S(1)} copy-done((f32[2048,512]{1,0:T(8,128)S(1)}, f32[2048,512]{1,0:T(8,128)}, u32[]{:S(2)}) %copy-start.4) | copy-done | bytes 4194328
  63.7 1.6 %copy-done.10 = f32[1024,512]{1,0:T(8,128)S(1)} copy-done((f32[1024,512]{1,0:T(8,128)S(1)}, f32[1024,512]{1,0:T(8,128)}, u32[]{:S(2)}) %copy-start.10) | copy-done | bytes 2097176
  65.3 1.2 copy-done.14
  66.5 1.2 copy-done.16
  67.7 5.4 %finish.4 = (f32[2048,512]{1,0:T(8,128)}, f32[2048,512]{1,0:T(8,128)}, f32[8,128]{1,0:T(8,128)S(1)}) custom-call(s32[7]{0:T(128)S(1)} %copy-done.24, s32[7,128]{1,0:T(8,128)S(1)} %copy-done.21, f32[1]{0:T(128)} %bitcast.1.shift, f32[512,512]{1,0:T(8,128)} %collective-permute-done.6.a0, f32[512,512]{1,0:T(8,128)S(1)} %copy-done.14, ...), custom_call_target="tpu_custom_call" | custom-call | flops 3221225472 | bytes 12582912 | tf_op jit(solution)/shard_map/finish/pallas_call | solution.py:348
  73.1 4.2 %collective-permute-done.13.a2 = f32[512,512]{1,0:T(8,128)} collective-permute-done((f32[512,512]{1,0:T(8,128)}, f32[512,512]{1,0:T(8,128)}, u32[]{:S(2)}, u32[]{:S(2)}) %collective-permute-start.13) | collective-permute-done | bytes 1048608 | tf_op jit(solution)/shard_map/ppermute | solution.py:40
  77.4 4.1 %collective-permute-start.21 = (f32[512,512]{1,0:T(8,128)}, f32[512,512]{1,0:T(8,128)S(1)}, u32[]{:S(2)}, u32[]{:S(2)}) collective-permute-start(f32[512,512]{1,0:T(8,128)} %collective-permute-done.13.a2), channel_id=1, source_target_pairs={{0,6},{1,73},{2,4},{3,75},{4,2},{5,77},{6,0},{7,79},{8,14},{9,65},... | collective-permute-start | bytes 3145736 | tf_op jit(solution)/shard_map/ppermute | solution.py:40
  81.4 1.5 %collective-permute-start = (f32[384,512]{1,0:T(8,128)S(1)}, f32[384,512]{1,0:T(8,128)}, u32[]{:S(2)}, u32[]{:S(2)}) collective-permute-start(f32[384,512]{1,0:T(8,128)S(1)} %copy-done.30), channel_id=1, source_target_pairs={{0,64},{1,17},{2,66},{3,19},{4,68},{5,21},{6,70},{7,23},{8,72},{9,... | collective-permute-start | bytes 2359304 | tf_op jit(solution)/shard_map/ppermute | solution.py:40
  82.9 2.1 %collective-permute-start.22 = (f32[640,512]{1,0:T(8,128)}, f32[640,512]{1,0:T(8,128)S(1)}, u32[]{:S(2)}, u32[]{:S(2)}) collective-permute-start(f32[640,512]{1,0:T(8,128)} %collective-permute-done.8.a0), channel_id=1, source_target_pairs={{0,72},{1,49},{2,74},{3,51},{4,76},{5,53},{6,78},{7,55},{8,64},{9,... | collective-permute-start | bytes 3932168 | tf_op jit(solution)/shard_map/ppermute | solution.py:40
  85.3 20.0 %collective-permute-done.21.b2 = f32[512,512]{1,0:T(8,128)S(1)} collective-permute-done((f32[512,512]{1,0:T(8,128)}, f32[512,512]{1,0:T(8,128)S(1)}, u32[]{:S(2)}, u32[]{:S(2)}) %collective-permute-start.21) | collective-permute-done | bytes 1048608 | tf_op jit(solution)/shard_map/ppermute | solution.py:40
  105.3 5.1 %finish.5 = (f32[2048,512]{1,0:T(8,128)}, f32[2048,512]{1,0:T(8,128)}, f32[8,128]{1,0:T(8,128)S(1)}) custom-call(s32[7]{0:T(128)S(1)} %copy-done.24, s32[7,128]{1,0:T(8,128)S(1)} %copy-done.21, f32[1]{0:T(128)} %bitcast.2.shift, f32[512,512]{1,0:T(8,128)S(1)} %collective-permute-done.11.a0, ...), custom_call_target="tpu_custom_call", output_to_operand_aliasing={{0}: (16, {}), {1}: (17, {})} | custom-call | flops 3221225472 | bytes 12582912 | tf_op jit(solution)/shard_map/finish/pallas_call | solution.py:348
  110.4 3.7 %collective-permute-start.24 = (f32[640,512]{1,0:T(8,128)S(1)}, f32[640,512]{1,0:T(8,128)S(1)}, u32[]{:S(2)}, u32[]{:S(2)}) collective-permute-start(f32[640,512]{1,0:T(8,128)S(1)} %collective-permute-done.10.a2), channel_id=1, source_target_pairs={{0,6},{1,73},{2,4},{3,75},{4,2},{5,77},{6,0},{7,79},{8,14},{9,65},... | collective-permute-start | bytes 3932168 | tf_op jit(solution)/shard_map/ppermute | solution.py:40
  114.1 1.3 collective-permute-start.2
  115.4 10.7 %collective-permute-done.2.a1 = f32[384,512]{1,0:T(8,128)S(1)} collective-permute-done((f32[384,512]{1,0:T(8,128)S(1)}, f32[384,512]{1,0:T(8,128)S(1)}, u32[]{:S(2)}, u32[]{:S(2)}) %collective-permute-start.2) | collective-permute-done | bytes 786464 | tf_op jit(solution)/shard_map/ppermute | solution.py:40
  126.1 2.3 %collective-permute-start.1 = (f32[384,512]{1,0:T(8,128)}, f32[384,512]{1,0:T(8,128)S(1)}, u32[]{:S(2)}, u32[]{:S(2)}) collective-permute-start(f32[384,512]{1,0:T(8,128)} %collective-permute-done.a0), channel_id=1, source_target_pairs={{0,72},{1,49},{2,74},{3,51},{4,76},{5,53},{6,78},{7,55},{8,64},{9,... | collective-permute-start | bytes 2359304 | tf_op jit(solution)/shard_map/ppermute | solution.py:40
  128.6 1.9 %copy-done.7 = f32[1024,512]{1,0:T(8,128)S(1)} copy-done((f32[1024,512]{1,0:T(8,128)S(1)}, f32[1024,512]{1,0:T(8,128)}, u32[]{:S(2)}) %copy-start.7) | copy-done | bytes 2097176
  130.5 3.5 %early.1.acc = f32[384,512]{1,0:T(8,128)S(1)} custom-call(s32[7]{0:T(128)S(1)} %copy-done.24, s32[7,128]{1,0:T(8,128)S(1)} %copy-done.21, f32[384,512]{1,0:T(8,128)} %collective-permute-done.a0, f32[384,512]{1,0:T(8,128)S(1)} %collective-permute-done.2.a1, f32[384,512]{1,0:T(8,128)S(1)} %collective-permute-done.4.a2, f32[2048,512]{1,0:T(8,128)S(1)} %copy-done.5, ...), custom_call_target="tpu_custom_call" | custom-call | flops 2147483648 | bytes 8388608 | tf_op jit(solution)/shard_map/early/pallas_call | solution.py:335
  134.0 4.1 %collective-permute-done.24.b2 = f32[640,512]{1,0:T(8,128)S(1)} collective-permute-done((f32[640,512]{1,0:T(8,128)S(1)}, f32[640,512]{1,0:T(8,128)S(1)}, u32[]{:S(2)}, u32[]{:S(2)}) %collective-permute-start.24) | collective-permute-done | bytes 1310752 | tf_op jit(solution)/shard_map/ppermute | solution.py:40
  138.1 1.3 copy-done.12
  139.4 7.0 %finish.6 = (f32[2048,512]{1,0:T(8,128)}, f32[2048,512]{1,0:T(8,128)}, f32[8,128]{1,0:T(8,128)S(1)}) custom-call(s32[7]{0:T(128)S(1)} %copy-done.24, s32[7,128]{1,0:T(8,128)S(1)} %copy-done.21, f32[1]{0:T(128)} %bitcast.3.shift, f32[640,512]{1,0:T(8,128)} %collective-permute-done.8.a0, ...), custom_call_target="tpu_custom_call", output_to_operand_aliasing={{0}: (16, {}), {1}: (17, {})} | custom-call | flops 3221225472 | bytes 12582912 | tf_op jit(solution)/shard_map/finish/pallas_call | solution.py:348
  146.5 3.1 %finish.7 = (f32[2048,512]{1,0:T(8,128)}, f32[2048,512]{1,0:T(8,128)}, f32[8,128]{1,0:T(8,128)}) custom-call(s32[7]{0:T(128)S(1)} %copy-done.24, s32[7,128]{1,0:T(8,128)S(1)} %copy-done.21, f32[1]{0:T(128)} %bitcast.4.shift, f32[384,512]{1,0:T(8,128)S(1)} %collective-permute-done.1.b0, ...), custom_call_target="tpu_custom_call", output_to_operand_aliasing={{0}: (12, {}), {1}: (13, {})} | custom-call | flops 3221225472 | bytes 12582912 | tf_op jit(solution)/shard_map/finish/pallas_call | solution.py:348
  (73 shorter events, 6.0 us)
Async XLA Ops:
  0.6 34.5 %collective-permute-start.7 = (f32[2048,512]{1,0:T(8,128)}, f32[2048,512]{1,0:T(8,128)S(1)}, u32[]{:S(2)}, u32[]{:S(2)}) collective-permute-start(f32[2048,512]{1,0:T(8,128)} %own.11), channel_id=1, source_target_pairs={{0,1},{1,0},{2,3},{3,2},{4,5},{5,4},{6,7},{7,6},{8,9},{9,8},{10,11... | collective-permute-start | bytes 12582920 | tf_op jit(solution)/shard_map/ppermute | solution.py:40
  2.0 24.0 %collective-permute-start.6 = (f32[512,512]{1,0:T(8,128)S(1)}, f32[512,512]{1,0:T(8,128)}, u32[]{:S(2)}, u32[]{:S(2)}) collective-permute-start(f32[512,512]{1,0:T(8,128)S(1)} %slice.3), channel_id=1, source_target_pairs={{0,64},{1,17},{2,66},{3,19},{4,68},{5,21},{6,70},{7,23},{8,72},{9,... | collective-permute-start | bytes 3145736 | tf_op jit(solution)/shard_map/ppermute | solution.py:40
  3.6 24.2 %collective-permute-start.14 = (f32[512,512]{1,0:T(8,128)S(1)}, f32[512,512]{1,0:T(8,128)S(1)}, u32[]{:S(2)}, u32[]{:S(2)}) collective-permute-start(f32[512,512]{1,0:T(8,128)S(1)} %slice.3), channel_id=1, source_target_pairs={{0,16},{1,3},{2,18},{3,1},{4,20},{5,7},{6,22},{7,5},{8,24},{9,11},... | collective-permute-start | bytes 3145736 | tf_op jit(solution)/shard_map/ppermute | solution.py:40
  4.9 24.8 %collective-permute-start.15 = (f32[512,512]{1,0:T(8,128)S(1)}, f32[512,512]{1,0:T(8,128)}, u32[]{:S(2)}, u32[]{:S(2)}) collective-permute-start(f32[512,512]{1,0:T(8,128)S(1)} %slice.3), channel_id=1, source_target_pairs={{0,2},{1,65},{2,0},{3,67},{4,6},{5,69},{6,4},{7,71},{8,10},{9,73},... | collective-permute-start | bytes 3145736 | tf_op jit(solution)/shard_map/ppermute | solution.py:40
  6.8 1.0 copy-start.17
  7.8 1.0 copy-start.18
  8.9 0.9 copy-start.19
  15.0 2.2 %copy-start = (f32[2048,512]{1,0:T(8,128)S(1)}, f32[2048,512]{1,0:T(8,128)}, u32[]{:S(2)}) copy-start(f32[2048,512]{1,0:T(8,128)} %own.11) | copy-start | bytes 12582916
  24.0 1.3 copy-start.9
  25.3 22.4 %collective-permute-start.11 = (f32[512,512]{1,0:T(8,128)}, f32[512,512]{1,0:T(8,128)S(1)}, u32[]{:S(2)}, u32[]{:S(2)}) collective-permute-start(f32[512,512]{1,0:T(8,128)} %get-tuple-element.40), channel_id=1, source_target_pairs={{0,64},{1,17},{2,66},{3,19},{4,68},{5,21},{6,70},{7,23},{8,72},{9,... | collective-permute-start | bytes 3145736 | tf_op jit(solution)/shard_map/ppermute | solution.py:40
  26.0 24.4 %collective-permute-start.12 = (f32[512,512]{1,0:T(8,128)}, f32[512,512]{1,0:T(8,128)}, u32[]{:S(2)}, u32[]{:S(2)}) collective-permute-start(f32[512,512]{1,0:T(8,128)} %get-tuple-element.40), channel_id=1, source_target_pairs={{0,16},{1,3},{2,18},{3,1},{4,20},{5,7},{6,22},{7,5},{8,24},{9,11},... | collective-permute-start | bytes 3145736 | tf_op jit(solution)/shard_map/ppermute | solution.py:40
  27.8 25.2 %collective-permute-start.17 = (f32[512,512]{1,0:T(8,128)S(1)}, f32[512,512]{1,0:T(8,128)S(1)}, u32[]{:S(2)}, u32[]{:S(2)}) collective-permute-start(f32[512,512]{1,0:T(8,128)S(1)} %collective-permute-done.14.a1), channel_id=1, source_target_pairs={{0,48},{1,7},{2,50},{3,5},{4,52},{5,3},{6,54},{7,1},{8,56},{9,15},... | collective-permute-start | bytes 3145736 | tf_op jit(solution)/shard_map/ppermute | solution.py:40
  28.7 1.0 copy-start.13
  29.7 26.7 %collective-permute-start.18 = (f32[512,512]{1,0:T(8,128)}, f32[512,512]{1,0:T(8,128)}, u32[]{:S(2)}, u32[]{:S(2)}) collective-permute-start(f32[512,512]{1,0:T(8,128)} %collective-permute-done.15.a2), channel_id=1, source_target_pairs={{0,6},{1,73},{2,4},{3,75},{4,2},{5,77},{6,0},{7,79},{8,14},{9,65},... | collective-permute-start | bytes 3145736 | tf_op jit(solution)/shard_map/ppermute | solution.py:40
  35.2 2.0 %copy-start.3 = (f32[2048,512]{1,0:T(8,128)}, f32[2048,512]{1,0:T(8,128)S(1)}, u32[]{:S(2)}) copy-start(f32[2048,512]{1,0:T(8,128)S(1)} %collective-permute-done.7.mate) | copy-start | bytes 12582916
  37.2 22.1 %copy-start.21 = (s32[7,128]{1,0:T(8,128)S(1)}, s32[7,128]{1,0:T(8,128)}, u32[]{:S(2)}) copy-start(s32[7,128]{1,0:T(8,128)} %signs_up.13) | copy-start | bytes 10756
  37.2 22.1 %copy-start.24 = (s32[7]{0:T(128)S(1)}, s32[7]{0:T(128)}, u32[]{:S(2)}) copy-start(s32[7]{0:T(128)} %bits_up.15) | copy-start | bytes 88
  37.2 22.1 %collective-permute-start.16 = (f32[512,512]{1,0:T(8,128)}, f32[512,512]{1,0:T(8,128)}, u32[]{:S(2)}, u32[]{:S(2)}) collective-permute-start(f32[512,512]{1,0:T(8,128)} %collective-permute-done.6.a0), channel_id=1, source_target_pairs={{0,72},{1,49},{2,74},{3,51},{4,76},{5,53},{6,78},{7,55},{8,64},{9,... | collective-permute-start | bytes 3145736 | tf_op jit(solution)/shard_map/ppermute | solution.py:40
  45.5 1.4 copy-start.6
  47.8 33.6 %collective-permute-start.8 = (f32[640,512]{1,0:T(8,128)}, f32[640,512]{1,0:T(8,128)}, u32[]{:S(2)}, u32[]{:S(2)}) collective-permute-start(f32[640,512]{1,0:T(8,128)} %get-tuple-element.39), channel_id=1, source_target_pairs={{0,64},{1,17},{2,66},{3,19},{4,68},{5,21},{6,70},{7,23},{8,72},{9,... | collective-permute-start | bytes 3932168 | tf_op jit(solution)/shard_map/ppermute | solution.py:40
  50.4 27.0 %collective-permute-start.13 = (f32[512,512]{1,0:T(8,128)}, f32[512,512]{1,0:T(8,128)}, u32[]{:S(2)}, u32[]{:S(2)}) collective-permute-start(f32[512,512]{1,0:T(8,128)} %get-tuple-element.40), channel_id=1, source_target_pairs={{0,2},{1,65},{2,0},{3,67},{4,6},{5,69},{6,4},{7,71},{8,10},{9,73},... | collective-permute-start | bytes 3145736 | tf_op jit(solution)/shard_map/ppermute | solution.py:40
  53.0 1.0 copy-start.15
  54.0 27.4 %collective-permute-start.9 = (f32[640,512]{1,0:T(8,128)}, f32[640,512]{1,0:T(8,128)}, u32[]{:S(2)}, u32[]{:S(2)}) collective-permute-start(f32[640,512]{1,0:T(8,128)} %get-tuple-element.39), channel_id=1, source_target_pairs={{0,16},{1,3},{2,18},{3,1},{4,20},{5,7},{6,22},{7,5},{8,24},{9,11},... | collective-permute-start | bytes 3932168 | tf_op jit(solution)/shard_map/ppermute | solution.py:40
  56.4 26.5 %collective-permute-start.19 = (f32[512,512]{1,0:T(8,128)S(1)}, f32[512,512]{1,0:T(8,128)S(1)}, u32[]{:S(2)}, u32[]{:S(2)}) collective-permute-start(f32[512,512]{1,0:T(8,128)S(1)} %collective-permute-done.11.a0), channel_id=1, source_target_pairs={{0,72},{1,49},{2,74},{3,51},{4,76},{5,53},{6,78},{7,55},{8,64},{9,... | collective-permute-start | bytes 3145736 | tf_op jit(solution)/shard_map/ppermute | solution.py:40
  59.3 25.8 %collective-permute-start.20 = (f32[512,512]{1,0:T(8,128)}, f32[512,512]{1,0:T(8,128)S(1)}, u32[]{:S(2)}, u32[]{:S(2)}) collective-permute-start(f32[512,512]{1,0:T(8,128)} %collective-permute-done.12.a1), channel_id=1, source_target_pairs={{0,48},{1,7},{2,50},{3,5},{4,52},{5,3},{6,54},{7,1},{8,56},{9,15},... | collective-permute-start | bytes 3145736 | tf_op jit(solution)/shard_map/ppermute | solution.py:40
  59.3 2.2 %copy-start.1 = (f32[2048,512]{1,0:T(8,128)S(1)}, f32[2048,512]{1,0:T(8,128)}, u32[]{:S(2)}) copy-start(f32[2048,512]{1,0:T(8,128)} %own.11) | copy-start | bytes 12582916
  61.5 2.2 %copy-start.4 = (f32[2048,512]{1,0:T(8,128)S(1)}, f32[2048,512]{1,0:T(8,128)}, u32[]{:S(2)}) copy-start(f32[2048,512]{1,0:T(8,128)} %copy-done.3) | copy-start | bytes 12582916
  63.7 1.6 %copy-start.10 = (f32[1024,512]{1,0:T(8,128)S(1)}, f32[1024,512]{1,0:T(8,128)}, u32[]{:S(2)}) copy-start(f32[1024,512]{1,0:T(8,128)} %copy-done.9) | copy-start | bytes 6291460
  65.3 1.2 copy-start.14
  66.5 1.2 copy-start.16
  67.7 13.7 %copy-start.30 = (f32[384,512]{1,0:T(8,128)S(1)}, f32[384,512]{1,0:T(8,128)}, u32[]{:S(2)}) copy-start(f32[384,512]{1,0:T(8,128)} %copy-done.29) | copy-start | bytes 2359300
  77.4 27.9 %collective-permute-start.21 = (f32[512,512]{1,0:T(8,128)}, f32[512,512]{1,0:T(8,128)S(1)}, u32[]{:S(2)}, u32[]{:S(2)}) collective-permute-start(f32[512,512]{1,0:T(8,128)} %collective-permute-done.13.a2), channel_id=1, source_target_pairs={{0,6},{1,73},{2,4},{3,75},{4,2},{5,77},{6,0},{7,79},{8,14},{9,65},... | collective-permute-start | bytes 3145736 | tf_op jit(solution)/shard_map/ppermute | solution.py:40
  81.4 29.0 %collective-permute-start.10 = (f32[640,512]{1,0:T(8,128)}, f32[640,512]{1,0:T(8,128)S(1)}, u32[]{:S(2)}, u32[]{:S(2)}) collective-permute-start(f32[640,512]{1,0:T(8,128)} %get-tuple-element.39), channel_id=1, source_target_pairs={{0,2},{1,65},{2,0},{3,67},{4,6},{5,69},{6,4},{7,71},{8,10},{9,73},... | collective-permute-start | bytes 3932168 | tf_op jit(solution)/shard_map/ppermute | solution.py:40
  81.4 33.9 %collective-permute-start = (f32[384,512]{1,0:T(8,128)S(1)}, f32[384,512]{1,0:T(8,128)}, u32[]{:S(2)}, u32[]{:S(2)}) collective-permute-start(f32[384,512]{1,0:T(8,128)S(1)} %copy-done.30), channel_id=1, source_target_pairs={{0,64},{1,17},{2,66},{3,19},{4,68},{5,21},{6,70},{7,23},{8,72},{9,... | collective-permute-start | bytes 2359304 | tf_op jit(solution)/shard_map/ppermute | solution.py:40
  82.9 45.4 %collective-permute-start.22 = (f32[640,512]{1,0:T(8,128)}, f32[640,512]{1,0:T(8,128)S(1)}, u32[]{:S(2)}, u32[]{:S(2)}) collective-permute-start(f32[640,512]{1,0:T(8,128)} %collective-permute-done.8.a0), channel_id=1, source_target_pairs={{0,72},{1,49},{2,74},{3,51},{4,76},{5,53},{6,78},{7,55},{8,64},{9,... | collective-permute-start | bytes 3932168 | tf_op jit(solution)/shard_map/ppermute | solution.py:40
  85.1 48.9 %collective-permute-start.23 = (f32[640,512]{1,0:T(8,128)}, f32[640,512]{1,0:T(8,128)}, u32[]{:S(2)}, u32[]{:S(2)}) collective-permute-start(f32[640,512]{1,0:T(8,128)} %collective-permute-done.9.a1), channel_id=1, source_target_pairs={{0,48},{1,7},{2,50},{3,5},{4,52},{5,3},{6,54},{7,1},{8,56},{9,15},... | collective-permute-start | bytes 3932168 | tf_op jit(solution)/shard_map/ppermute | solution.py:40
  105.3 23.3 %copy-start.5 = (f32[2048,512]{1,0:T(8,128)S(1)}, f32[2048,512]{1,0:T(8,128)}, u32[]{:S(2)}) copy-start(f32[2048,512]{1,0:T(8,128)} %copy-done.3) | copy-start | bytes 12582916
  110.4 27.7 %collective-permute-start.24 = (f32[640,512]{1,0:T(8,128)S(1)}, f32[640,512]{1,0:T(8,128)S(1)}, u32[]{:S(2)}, u32[]{:S(2)}) collective-permute-start(f32[640,512]{1,0:T(8,128)S(1)} %collective-permute-done.10.a2), channel_id=1, source_target_pairs={{0,6},{1,73},{2,4},{3,75},{4,2},{5,77},{6,0},{7,79},{8,14},{9,65},... | collective-permute-start | bytes 3932168 | tf_op jit(solution)/shard_map/ppermute | solution.py:40
  114.1 12.0 %collective-permute-start.2 = (f32[384,512]{1,0:T(8,128)S(1)}, f32[384,512]{1,0:T(8,128)S(1)}, u32[]{:S(2)}, u32[]{:S(2)}) collective-permute-start(f32[384,512]{1,0:T(8,128)S(1)} %copy-done.30), channel_id=1, source_target_pairs={{0,16},{1,3},{2,18},{3,1},{4,20},{5,7},{6,22},{7,5},{8,24},{9,11},... | collective-permute-start | bytes 2359304 | tf_op jit(solution)/shard_map/ppermute | solution.py:40
  115.4 13.0 %collective-permute-start.4 = (f32[384,512]{1,0:T(8,128)S(1)}, f32[384,512]{1,0:T(8,128)S(1)}, u32[]{:S(2)}, u32[]{:S(2)}) collective-permute-start(f32[384,512]{1,0:T(8,128)S(1)} %copy-done.30), channel_id=1, source_target_pairs={{0,2},{1,65},{2,0},{3,67},{4,6},{5,69},{6,4},{7,71},{8,10},{9,73},... | collective-permute-start | bytes 2359304 | tf_op jit(solution)/shard_map/ppermute | solution.py:40
  126.1 20.3 %collective-permute-start.1 = (f32[384,512]{1,0:T(8,128)}, f32[384,512]{1,0:T(8,128)S(1)}, u32[]{:S(2)}, u32[]{:S(2)}) collective-permute-start(f32[384,512]{1,0:T(8,128)} %collective-permute-done.a0), channel_id=1, source_target_pairs={{0,72},{1,49},{2,74},{3,51},{4,76},{5,53},{6,78},{7,55},{8,64},{9,... | collective-permute-start | bytes 2359304 | tf_op jit(solution)/shard_map/ppermute | solution.py:40
  128.4 18.0 %collective-permute-start.3 = (f32[384,512]{1,0:T(8,128)S(1)}, f32[384,512]{1,0:T(8,128)S(1)}, u32[]{:S(2)}, u32[]{:S(2)}) collective-permute-start(f32[384,512]{1,0:T(8,128)S(1)} %collective-permute-done.2.a1), channel_id=1, source_target_pairs={{0,48},{1,7},{2,50},{3,5},{4,52},{5,3},{6,54},{7,1},{8,56},{9,15},... | collective-permute-start | bytes 2359304 | tf_op jit(solution)/shard_map/ppermute | solution.py:40
  128.4 5.6 %copy-start.11 = (f32[640,512]{1,0:T(8,128)}, f32[640,512]{1,0:T(8,128)S(1)}, u32[]{:S(2)}) copy-start(f32[640,512]{1,0:T(8,128)S(1)} %collective-permute-done.22.b0) | copy-start | bytes 3932164
  128.4 18.1 %collective-permute-start.5 = (f32[384,512]{1,0:T(8,128)S(1)}, f32[384,512]{1,0:T(8,128)S(1)}, u32[]{:S(2)}, u32[]{:S(2)}) collective-permute-start(f32[384,512]{1,0:T(8,128)S(1)} %collective-permute-done.4.a2), channel_id=1, source_target_pairs={{0,6},{1,73},{2,4},{3,75},{4,2},{5,77},{6,0},{7,79},{8,14},{9,65},... | collective-permute-start | bytes 2359304 | tf_op jit(solution)/shard_map/ppermute | solution.py:40
  128.6 1.9 %copy-start.7 = (f32[1024,512]{1,0:T(8,128)S(1)}, f32[1024,512]{1,0:T(8,128)}, u32[]{:S(2)}) copy-start(f32[1024,512]{1,0:T(8,128)} %copy-done.6) | copy-start | bytes 6291460
  130.5 7.6 %copy-start.2 = (f32[2048,512]{1,0:T(8,128)S(1)}, f32[2048,512]{1,0:T(8,128)}, u32[]{:S(2)}) copy-start(f32[2048,512]{1,0:T(8,128)} %own.11) | copy-start | bytes 12582916
  130.5 7.6 %copy-start.8 = (f32[1024,512]{1,0:T(8,128)S(1)}, f32[1024,512]{1,0:T(8,128)}, u32[]{:S(2)}) copy-start(f32[1024,512]{1,0:T(8,128)} %copy-done.6) | copy-start | bytes 6291460
  138.1 1.3 copy-start.12
  (8 other events, 5.6 us)
